TPU v7x, 128 devices: a whole 4x4x4 slice. The times are simulated.
128 devices in a mesh: seq: 4 (over z), chan: 32 (over x, y, core).
Axes of the slice: x: 4, y: 4, z: 4, core: 2. Of those that a mesh axis runs over, the one named last changes fastest.
Arguments:
- query_rows: bfloat16 [16384, 4096], P(('seq', 'chan')), may hold values from -6 to 6
- key_rows: bfloat16 [16384, 4096], P(('seq', 'chan')), may hold values from -6 to 6
- value_rows: bfloat16 [16384, 4096], P(('seq', 'chan')), may hold values from -6 to 6
- residue: float32 [4096, 16], P('chan'), may hold values from -1.5 to 1.5
- pole_rate: float32 [4096, 16], P('chan'), may hold values from 1 to 512
- skip_gain: float32 [4096], P('chan'), may hold values from -4 to 4
- out_weight: bfloat16 [4096, 4096], P('chan', 'seq'), may hold values from -0.09375 to 0.09375
Outputs:
- projected: bfloat16 [4, 4096, 4096], P(None, 'chan', 'seq')
All inputs are finite; a program needn't handle non-finite values.
Results may differ from a plain program's by a relative error of at most 0.014.
Values may be sent and summed in bfloat16 or wider, within the bound.
No kernel may reach another device: no remote copies, remote signals or barrier semaphores. Data moves between devices by JAX's collectives and lax.ppermute only.
A program may use at most 192 MiB of HBM per device.

v0:
```python
import math

import jax
import jax.numpy as jnp
from jax import lax
from jax.sharding import PartitionSpec as P

SPANS = 16


precise = lax.Precision.HIGHEST
three_pass = lax.Precision.HIGH


def forward_matrix(block_len):
    frequency = jnp.arange(block_len, dtype=jnp.int32)
    position = jnp.arange(block_len, dtype=jnp.int32)
    phases = frequency[:, None] * position[None, :] % (2 * block_len)
    angles = phases.astype(jnp.float32) * (math.pi / block_len)
    real_rows = jnp.cos(angles)
    alternate = jnp.where(position % 2 == 0, 1.0, -1.0).astype(jnp.float32)
    imag_rows = jnp.where(frequency[:, None] == 0, alternate[None, :], -jnp.sin(angles))
    return jnp.concatenate([real_rows, imag_rows], axis=0)


def split_matrix(matrix):
    upper_part = matrix.astype(jnp.bfloat16)
    lower_part = (matrix - upper_part.astype(jnp.float32)).astype(jnp.bfloat16)
    return (upper_part, lower_part)


def inverse_matrix(block_len):
    outputs = jnp.arange(block_len, dtype=jnp.int32) + block_len
    frequency = jnp.arange(block_len, dtype=jnp.int32)
    phases = outputs[:, None] * frequency[None, :] % (2 * block_len)
    angles = phases.astype(jnp.float32) * (math.pi / block_len)
    scaling = jnp.where(frequency[None, :] == 0, 1.0, 2.0).astype(jnp.float32) / (2.0 * block_len)
    real_cols = scaling * jnp.cos(angles)
    alternate = (jnp.where(outputs % 2 == 0, 1.0, -1.0).astype(jnp.float32) / (2.0 * block_len))[
        :, None
    ]
    imag_cols = jnp.where(frequency[None, :] == 0, alternate, -scaling * jnp.sin(angles))
    return jnp.concatenate([real_cols, imag_cols], axis=1)


def pole_spectra(decay_rate, block_len):
    frequency = jnp.arange(block_len, dtype=jnp.int32)
    angles = (frequency.astype(jnp.float32) * (math.pi / block_len))[:, None, None]
    retain = jnp.exp(-decay_rate)[None]
    leakage = -jnp.expm1(-decay_rate)[None]
    real_den = 2.0 * jnp.square(jnp.sin(0.5 * angles)) + leakage * jnp.cos(angles)
    imag_den = retain * jnp.sin(angles)
    modulus = real_den * real_den + imag_den * imag_den
    real_part = real_den / modulus
    imag_part = jnp.where(frequency[:, None, None] == 0, 1.0 / (1.0 + retain), -imag_den / modulus)
    return jnp.concatenate([real_part, imag_part], axis=0)


def lag_spectra(pole_terms, plain_sum, weight, decay_rate, lag_steps, block_len):
    lag_float = lag_steps.astype(jnp.float32)[:, None, None]
    later = (
        weight[None]
        * jnp.exp(-decay_rate[None] * (block_len * jnp.maximum(lag_float - 1.0, 0.0)))
        * (-jnp.expm1(-2.0 * block_len * decay_rate))[None]
    )
    first = -weight * jnp.exp(-decay_rate * block_len)
    lag_weight = jnp.where(lag_float >= 1.0, later, jnp.where(lag_float == 0.0, first[None], 0.0))
    summed = jnp.einsum("kcm,rcm->krc", pole_terms, lag_weight, precision=precise)
    parity = jnp.where(jnp.arange(2 * block_len) % 2 == 0, 1.0, -1.0).astype(jnp.float32)
    at_zero = (lag_steps == 0).astype(jnp.float32)
    return summed + parity[:, None, None] * at_zero[None, :, None] * plain_sum[:, None, :]


def packed_product(left_side, right_side, block_len):
    column_shape = (block_len,) + (1,) * (left_side.ndim - 1)
    inner_mask = (jnp.arange(block_len) > 0).astype(jnp.float32).reshape(column_shape)
    left_real, left_imag = (left_side[:block_len], left_side[block_len:])
    right_real, right_imag = (right_side[:block_len], right_side[block_len:])
    real_out = left_real * right_real - inner_mask * left_imag * right_imag
    cross_term = left_real * right_imag + left_imag * right_real
    imag_out = inner_mask * cross_term + (1.0 - inner_mask) * left_imag * right_imag
    return jnp.concatenate([real_out, imag_out], axis=0)


def to_spectra(signal_bf, matrix_pair, block_len):
    seq_rows, channels = signal_bf.shape
    block_count = seq_rows // block_len
    arranged = (
        signal_bf.reshape(block_count, block_len, channels)
        .transpose(1, 0, 2)
        .reshape(block_len, block_count * channels)
    )
    spectrum = jnp.dot(matrix_pair[0], arranged, preferred_element_type=jnp.float32)
    spectrum = spectrum + jnp.dot(matrix_pair[1], arranged, preferred_element_type=jnp.float32)
    return spectrum.reshape(2 * block_len, block_count, channels)


def from_spectra(spectrum, matrix, block_len):
    block_count, channels = (spectrum.shape[1], spectrum.shape[2])
    flat = jnp.dot(
        matrix,
        spectrum.reshape(2 * block_len, block_count * channels),
        precision=three_pass,
        preferred_element_type=jnp.float32,
    )
    return (
        flat.reshape(block_len, block_count, channels)
        .transpose(1, 0, 2)
        .reshape(block_count * block_len, channels)
    )


def on_device(query_rows, key_rows, value_rows, residue, pole_rate, skip_gain, out_weight):
    product = (key_rows.astype(jnp.float32) * value_rows.astype(jnp.float32)).astype(jnp.bfloat16)
    received = lax.all_to_all(product, "chan", split_axis=1, concat_axis=0, tiled=True)
    seq_rows, channels = received.shape
    seq_count = lax.axis_size("seq")
    block_len = seq_rows * seq_count // SPANS
    own_count = seq_rows // block_len
    own_index = lax.axis_index("seq")
    own_first = own_index * own_count
    signal = received.astype(jnp.float32)
    decay_rate = pole_rate / (seq_rows * seq_count)
    weight = residue * jnp.sqrt(2.0 * decay_rate)
    pole_terms = pole_spectra(decay_rate, block_len)
    plain_sum = jnp.einsum("kcm,cm->kc", pole_terms, weight, precision=precise)
    forward = split_matrix(forward_matrix(block_len))
    inverse = inverse_matrix(block_len)
    zero_spectra = jnp.zeros((2 * block_len, own_count, channels), jnp.float32)
    piece_rows = lax.all_gather(received, "seq", axis=0, tiled=True)

    def make_spectrum():
        return to_spectra(piece_rows, forward, block_len)

    block_count = piece_rows.shape[0] // block_len

    def process(partial_value):
        spectrum = make_spectrum()
        lag_steps = (
            own_first - (block_count - 1) + jnp.arange(own_count + block_count - 1, dtype=jnp.int32)
        )
        lagged = lag_spectra(pole_terms, plain_sum, weight, decay_rate, lag_steps, block_len)

        def one_source(source_index, inner_sum):
            window = lax.dynamic_slice_in_dim(lagged, block_count - 1 - source_index, own_count, 1)
            source = lax.dynamic_index_in_dim(spectrum, source_index, 1, keepdims=True)
            return inner_sum + packed_product(window, source, block_len)

        return lax.fori_loop(0, block_count, one_source, partial_value)

    def unchanged(partial_value):
        return partial_value

    gathered = lax.cond(
        jnp.int32(0) // block_len < own_first + own_count, process, unchanged, zero_spectra
    )
    convolved = from_spectra(gathered, inverse, block_len)
    mixed = (convolved + skip_gain[None, :] * signal).astype(jnp.bfloat16)
    regrouped = lax.all_to_all(mixed, "chan", split_axis=0, concat_axis=1, tiled=True)
    gated = (query_rows.astype(jnp.float32) * regrouped.astype(jnp.float32)).astype(jnp.bfloat16)
    token_block = lax.all_gather(gated, "seq", axis=0, tiled=True)
    result = jnp.dot(
        token_block,
        lax.all_gather(out_weight, "chan", axis=0, tiled=True),
        preferred_element_type=jnp.float32,
    )
    return result.astype(jnp.bfloat16).reshape(seq_count, query_rows.shape[0], out_weight.shape[1])


def solution(mesh):
    in_specs = (
        P(("seq", "chan"), None),
        P(("seq", "chan"), None),
        P(("seq", "chan"), None),
        P("chan", None),
        P("chan", None),
        P("chan"),
        P("chan", "seq"),
    )
    out_specs = P(None, "chan", "seq")
    return jax.shard_map(
        on_device, mesh=mesh, in_specs=in_specs, out_specs=out_specs, check_vma=False
    )
```

profile of v0, /device:TPU:0, one launch (start us, length us, event | category | flops | bytes accessed | tf_op | source)
XLA Modules:
  0.0 882.8 jit_solution(517808230430025885)
XLA Ops:
  8.4 24.1 %all_to_all.29 = bf16[128,32,128]{2,0,1:T(8,128)(2,1)} all-to-all(bf16[128,32,128]{2,0,1:T(8,128)(2,1)S(1)} %copy_bitcast_fusion), channel_id=1, replica_groups=mesh['seq'=4,'chan'=32] {'chan'}, dimensions={1} | all-to-all | bytes 2097152 | tf_op jit(solution)/shard_map/all_to_all | solution.py:115
  37.0 10.1 %fusion.55 = f32[128,1,2048]{2,1,0:T(1,128)} fusion(f32[128,16,1]{1,2,0:T(1,128)S(1)} %copy.44, f32[1024,128,16]{0,2,1:T(8,128)S(1)} %get-tuple-element.201, f32[1024,128,16]{0,2,1:T(8,128)S(1)} %get-tuple-element.200), kind=kOutput, calls=%fused_computation.116 | convolution fusion | flops 54525952 | bytes 17833984 | tf_op jit(solution)/shard_map/kcm,cm->kc/dot_general | solution.py:126
  48.7 16.2 %fusion.42 = f32[1024,1024]{1,0:T(8,128)} fusion(), kind=kLoop, calls=%fused_computation.84 | loop fusion | flops 14680064 | bytes 4194304 | tf_op jit(solution)/shard_map/cos | solution.py:20
  64.9 34.7 %cosine_multiply_fusion = (f32[1024,1024]{1,0:T(8,128)}, f32[1024,1024]{1,0:T(8,128)}, f32[1024,1024]{1,0:T(8,128)S(1)}) fusion(s32[1024]{0:T(1024)S(1)} %iota_add_fusion.1, f32[1024]{0:T(1024)S(1)} %get-tuple-element.212, f32[1024]{0:T(1024)S(1)} %get-tuple-element.214, f32[1024]{0:T(1024)S(1)} %get-tuple-element.211, ...), kind=kLoop, calls=%fused_computation.74 | loop fusion | flops 34603008 | bytes 12604416 | tf_op jit(solution)/shard_map/mul | solution.py:38
  120.5 599.2 %conditional.1 = (f32[2048,4,128]{2,1,0:T(4,128)}) conditional(s32[]{:T(128)} %convert_element_type.122, () %tuple.33, (s32[]{:T(128)}, f32[128,16]{0,1:T(8,128)S(1)}, f32[128,16]{1,0:T(8,128)S(1)}, f32[2048,128,16]{0,2,1:T(8,128)}, f32[2048,128]{0,1:T(8,128)S(1)}, /*index=5*/bf16[16384,128]{1,0:T(8,128)(2,1)}, bf16[2048,1024]{1,0:T(8,128)(2,1)}, ...), branch_computations={%region_0.1_spmd, %region_1.4_spmd} | conditional | flops 18159507456 | bytes 190227168 | solution.py:154
  120.8 31.7 %bitcast_add_fusion = f32[2048,19,128]{0,1,2:T(8,128)} fusion(f32[2048,128]{0,1:T(8,128)S(1)} %get-tuple-element.137, f32[2048,19]{0,1:T(8,128)S(1)} %broadcast_multiply_fusion, f32[2048,128,16]{0,2,1:T(8,128)} %get-tuple-element.136, f32[128,16]{1,0:T(8,128)S(1)} %get-tuple-element.196, f32[128,16]{1,0:T(8,128)S(1)} %get-tuple-element.197, ...), kind=kOutput, calls=%fused_computation.10 | convolution fusion | flops 966457344 | bytes 37937264 | tf_op jit(solution)/shard_map/cond/branch_1_fun/kcm,rcm->krc/dot_general | solution.py:68
  159.0 15.3 %fusion.57 = f32[2048,2048]{0,1:T(8,128)} fusion(bf16[2048,1024]{1,0:T(8,128)(2,1)} %get-tuple-element.138, bf16[1024,2048]{0,1:T(8,128)(2,1)} %bitcast.74), kind=kOutput, calls=%fused_computation.118 | convolution fusion | flops 8589934592 | bytes 25165824 | tf_op jit(solution)/shard_map/cond/branch_1_fun/dot_general | solution.py:93
  174.3 17.3 %convolution_add_fusion = f32[2048,2048]{0,1:T(8,128)} fusion(f32[2048,2048]{0,1:T(8,128)} %fusion.57, bf16[2048,1024]{1,0:T(8,128)(2,1)S(1)} %copy-done.4, bf16[1024,2048]{0,1:T(8,128)(2,1)S(1)} %bitcast.75), kind=kOutput, calls=%fused_computation.11 | convolution fusion | flops 8594128896 | bytes 41943040 | tf_op jit(solution)/shard_map/cond/branch_1_fun/dot_general | solution.py:94
  191.6 528.1 %while.15 = (s32[]{:T(128)}, f32[2048,4,128]{2,1,0:T(4,128)}, f32[2048,19,128]{0,1,2:T(8,128)}, f32[2048,16,128]{0,2,1:T(8,128)}, s32[]{:T(128)}, /*index=5*/s32[]{:T(128)}, s32[]{:T(128)}, s32[]{:T(128)}, s32[]{}) while((s32[]{:T(128)}, f32[2048,4,128]{2,1,0:T(4,128)}, f32[2048,19,128]{0,1,2:T(8,128)}, ...), condition=%wide.region_3.3_spmd.clone, body=%wide.region_2.2_spmd.clone.sunk | while | flops 8918024 | bytes 43008176 | solution.py:149
  240.1 9.3 %multiply_subtract_fusion.2 = (f32[1024,4,128]{2,1,0:T(4,128)S(1)}, f32[1024,4,128]{2,1,0:T(4,128)}) fusion(f32[1024,4,128]{2,1,0:T(4,128)} %copy.65, f32[1024,4,128]{2,1,0:T(4,128)} %copy.66, f32[1024,128]{1,0:T(8,128)S(1)} %bitcast.67, f32[1024]{0:T(1024)S(1)} %fusion.72, f32[1024,128]{1,0:T(8,128)S(1)} %bitcast.68, ...), kind=kLoop, calls=%fused_computation.2.clone.1 | loop fusion | flops 5767168 | bytes 9445376 | tf_op jit(solution)/shard_map/cond/branch_1_fun/while/body/eval_jaxpr/sub | solution.py:79
  273.1 9.3 %multiply_subtract_fusion.2 = (f32[1024,4,128]{2,1,0:T(4,128)S(1)}, f32[1024,4,128]{2,1,0:T(4,128)}) fusion(f32[1024,4,128]{2,1,0:T(4,128)} %copy.65, f32[1024,4,128]{2,1,0:T(4,128)} %copy.66, f32[1024,128]{1,0:T(8,128)S(1)} %bitcast.67, f32[1024]{0:T(1024)S(1)} %fusion.72, f32[1024,128]{1,0:T(8,128)S(1)} %bitcast.68, ...), kind=kLoop, calls=%fused_computation.2.clone.1 | loop fusion | flops 5767168 | bytes 9445376 | tf_op jit(solution)/shard_map/cond/branch_1_fun/while/body/eval_jaxpr/sub | solution.py:79
  306.2 9.3 %multiply_subtract_fusion.2 = (f32[1024,4,128]{2,1,0:T(4,128)S(1)}, f32[1024,4,128]{2,1,0:T(4,128)}) fusion(f32[1024,4,128]{2,1,0:T(4,128)} %copy.65, f32[1024,4,128]{2,1,0:T(4,128)} %copy.66, f32[1024,128]{1,0:T(8,128)S(1)} %bitcast.67, f32[1024]{0:T(1024)S(1)} %fusion.72, f32[1024,128]{1,0:T(8,128)S(1)} %bitcast.68, ...), kind=kLoop, calls=%fused_computation.2.clone.1 | loop fusion | flops 5767168 | bytes 9445376 | tf_op jit(solution)/shard_map/cond/branch_1_fun/while/body/eval_jaxpr/sub | solution.py:79
  339.3 9.3 %multiply_subtract_fusion.2 = (f32[1024,4,128]{2,1,0:T(4,128)S(1)}, f32[1024,4,128]{2,1,0:T(4,128)}) fusion(f32[1024,4,128]{2,1,0:T(4,128)} %copy.65, f32[1024,4,128]{2,1,0:T(4,128)} %copy.66, f32[1024,128]{1,0:T(8,128)S(1)} %bitcast.67, f32[1024]{0:T(1024)S(1)} %fusion.72, f32[1024,128]{1,0:T(8,128)S(1)} %bitcast.68, ...), kind=kLoop, calls=%fused_computation.2.clone.1 | loop fusion | flops 5767168 | bytes 9445376 | tf_op jit(solution)/shard_map/cond/branch_1_fun/while/body/eval_jaxpr/sub | solution.py:79
  372.4 9.3 %multiply_subtract_fusion.2 = (f32[1024,4,128]{2,1,0:T(4,128)S(1)}, f32[1024,4,128]{2,1,0:T(4,128)}) fusion(f32[1024,4,128]{2,1,0:T(4,128)} %copy.65, f32[1024,4,128]{2,1,0:T(4,128)} %copy.66, f32[1024,128]{1,0:T(8,128)S(1)} %bitcast.67, f32[1024]{0:T(1024)S(1)} %fusion.72, f32[1024,128]{1,0:T(8,128)S(1)} %bitcast.68, ...), kind=kLoop, calls=%fused_computation.2.clone.1 | loop fusion | flops 5767168 | bytes 9445376 | tf_op jit(solution)/shard_map/cond/branch_1_fun/while/body/eval_jaxpr/sub | solution.py:79
  405.5 9.3 %multiply_subtract_fusion.2 = (f32[1024,4,128]{2,1,0:T(4,128)S(1)}, f32[1024,4,128]{2,1,0:T(4,128)}) fusion(f32[1024,4,128]{2,1,0:T(4,128)} %copy.65, f32[1024,4,128]{2,1,0:T(4,128)} %copy.66, f32[1024,128]{1,0:T(8,128)S(1)} %bitcast.67, f32[1024]{0:T(1024)S(1)} %fusion.72, f32[1024,128]{1,0:T(8,128)S(1)} %bitcast.68, ...), kind=kLoop, calls=%fused_computation.2.clone.1 | loop fusion | flops 5767168 | bytes 9445376 | tf_op jit(solution)/shard_map/cond/branch_1_fun/while/body/eval_jaxpr/sub | solution.py:79
  438.5 9.3 %multiply_subtract_fusion.2 = (f32[1024,4,128]{2,1,0:T(4,128)S(1)}, f32[1024,4,128]{2,1,0:T(4,128)}) fusion(f32[1024,4,128]{2,1,0:T(4,128)} %copy.65, f32[1024,4,128]{2,1,0:T(4,128)} %copy.66, f32[1024,128]{1,0:T(8,128)S(1)} %bitcast.67, f32[1024]{0:T(1024)S(1)} %fusion.72, f32[1024,128]{1,0:T(8,128)S(1)} %bitcast.68, ...), kind=kLoop, calls=%fused_computation.2.clone.1 | loop fusion | flops 5767168 | bytes 9445376 | tf_op jit(solution)/shard_map/cond/branch_1_fun/while/body/eval_jaxpr/sub | solution.py:79
  471.7 9.3 %multiply_subtract_fusion.2 = (f32[1024,4,128]{2,1,0:T(4,128)S(1)}, f32[1024,4,128]{2,1,0:T(4,128)}) fusion(f32[1024,4,128]{2,1,0:T(4,128)} %copy.65, f32[1024,4,128]{2,1,0:T(4,128)} %copy.66, f32[1024,128]{1,0:T(8,128)S(1)} %bitcast.67, f32[1024]{0:T(1024)S(1)} %fusion.72, f32[1024,128]{1,0:T(8,128)S(1)} %bitcast.68, ...), kind=kLoop, calls=%fused_computation.2.clone.1 | loop fusion | flops 5767168 | bytes 9445376 | tf_op jit(solution)/shard_map/cond/branch_1_fun/while/body/eval_jaxpr/sub | solution.py:79
  504.8 9.3 %multiply_subtract_fusion.2 = (f32[1024,4,128]{2,1,0:T(4,128)S(1)}, f32[1024,4,128]{2,1,0:T(4,128)}) fusion(f32[1024,4,128]{2,1,0:T(4,128)} %copy.65, f32[1024,4,128]{2,1,0:T(4,128)} %copy.66, f32[1024,128]{1,0:T(8,128)S(1)} %bitcast.67, f32[1024]{0:T(1024)S(1)} %fusion.72, f32[1024,128]{1,0:T(8,128)S(1)} %bitcast.68, ...), kind=kLoop, calls=%fused_computation.2.clone.1 | loop fusion | flops 5767168 | bytes 9445376 | tf_op jit(solution)/shard_map/cond/branch_1_fun/while/body/eval_jaxpr/sub | solution.py:79
  537.9 9.3 %multiply_subtract_fusion.2 = (f32[1024,4,128]{2,1,0:T(4,128)S(1)}, f32[1024,4,128]{2,1,0:T(4,128)}) fusion(f32[1024,4,128]{2,1,0:T(4,128)} %copy.65, f32[1024,4,128]{2,1,0:T(4,128)} %copy.66, f32[1024,128]{1,0:T(8,128)S(1)} %bitcast.67, f32[1024]{0:T(1024)S(1)} %fusion.72, f32[1024,128]{1,0:T(8,128)S(1)} %bitcast.68, ...), kind=kLoop, calls=%fused_computation.2.clone.1 | loop fusion | flops 5767168 | bytes 9445376 | tf_op jit(solution)/shard_map/cond/branch_1_fun/while/body/eval_jaxpr/sub | solution.py:79
  729.9 10.7 %fusion.24 = f32[1024,4,128]{2,0,1:T(8,128)S(1)} fusion(f32[4,128,2048]{2,1,0:T(8,128)} %bitcast.73, f32[1024,1024]{1,0:T(8,128)} %get-tuple-element.207, f32[1024,1024]{1,0:T(8,128)} %get-tuple-element.206), kind=kOutput, calls=%fused_computation.49 | convolution fusion | flops 6444548096 | bytes 14680064 | tf_op jit(solution)/shard_map/dot_general | solution.py:100
  741.0 20.7 %all_to_all.30 = bf16[32,128,128]{2,1,0:T(8,128)(2,1)S(1)} all-to-all(bf16[32,128,128]{2,1,0:T(8,128)(2,1)S(1)} %add_convert_fusion), channel_id=1, replica_groups=mesh['seq'=4,'chan'=32] {'chan'}, dimensions={0} | all-to-all | bytes 2097152 | tf_op jit(solution)/shard_map/all_to_all | solution.py:159
  763.7 47.0 %all-gather.6.cloned.1.call-done = bf16[512,4096]{1,0:T(8,128)(2,1)} async-done(((bf16[128,4096]{1,0:T(8,128)(2,1)}), bf16[512,4096]{1,0:T(8,128)(2,1)}) %all-gather.6.cloned.1.call-update) | async-done | bytes 4194320 | tf_op jit(solution)/shard_map/all_gather | solution.py:161
  810.7 55.2 %all-gather.8.cloned.1.call-done = bf16[4096,1024]{1,0:T(8,128)(2,1)} async-done(((bf16[128,1024]{1,0:T(8,128)(2,1)}), bf16[4096,1024]{1,0:T(8,128)(2,1)}) %all-gather.8.cloned.1.call-update) | async-done | bytes 8388624 | tf_op jit(solution)/shard_map/all_gather | solution.py:164
  865.9 10.1 %convolution_convert_fusion = bf16[512,1024]{1,0:T(8,128)(2,1)} fusion(bf16[512,4096]{1,0:T(8,128)(2,1)} %all-gather.6.cloned.1.call-done, bf16[4096,1024]{1,0:T(8,128)(2,1)} %all-gather.8.cloned.1.call-done), kind=kOutput, calls=%fused_computation.85 | convolution fusion | flops 4295491584 | bytes 13631488 | tf_op jit(solution)/shard_map/dot_general | solution.py:162
  (218 shorter events, 482.3 us)
Async XLA Ops:
  6.5 26.1 %copy-start.8 = (f32[128,16]{0,1:T(8,128)S(1)}, f32[128,16]{0,1:T(8,128)}, u32[]{:S(2)}) copy-start(f32[128,16]{0,1:T(8,128)} %param.15) | copy-start | bytes 24580
  6.5 26.1 %copy-start.9 = (f32[128,16]{0,1:T(8,128)S(1)}, f32[128,16]{0,1:T(8,128)}, u32[]{:S(2)}) copy-start(f32[128,16]{0,1:T(8,128)} %param.14) | copy-start | bytes 24580
  6.5 114.0 %all-gather.4.cloned.1.call-start = ((), (), s32[]{:S(2)}) async-start(), calls=%async_computation.2 | async-start | bytes 5242880 | tf_op jit(solution)/shard_map/all_gather | solution.py:130
  32.6 778.1 %all-gather.6.cloned.1.call-start = ((), (), s32[]{:S(2)}) async-start(), calls=%async_computation.3 | async-start | bytes 5242880 | tf_op jit(solution)/shard_map/all_gather | solution.py:161
  37.0 10.1 %copy-start = (f32[1024,128,16]{0,2,1:T(8,128)}, f32[1024,128,16]{0,2,1:T(8,128)S(1)}, u32[]{:S(2)}) copy-start(f32[1024,128,16]{0,2,1:T(8,128)S(1)} %get-tuple-element.200) | copy-start | bytes 25165828
  37.0 10.1 %copy-start.1 = (f32[1024,128,16]{0,2,1:T(8,128)}, f32[1024,128,16]{0,2,1:T(8,128)S(1)}, u32[]{:S(2)}) copy-start(f32[1024,128,16]{0,2,1:T(8,128)S(1)} %get-tuple-element.201) | copy-start | bytes 25165828
  99.6 2.0 copy-start.2
  101.7 10.8 %slice-start = ((s8[8388608]{0:T(1024)(128)(4,1)}), s8[4194304]{0:T(1024)(128)(4,1)S(1)}, s32[]{:S(2)}) async-start(s8[8388608]{0:T(1024)(128)(4,1)} %bitcast.63), calls=%async_computation.5 | async-start | bytes 8388608
  101.7 10.8 %slice-start.2 = ((s8[8388608]{0:T(1024)(128)(4,1)}), s8[4194304]{0:T(1024)(128)(4,1)S(1)}, s32[]{:S(2)}) async-start(s8[8388608]{0:T(1024)(128)(4,1)} %bitcast.65), calls=%async_computation.7 | async-start | bytes 8388608
  106.8 6.4 slice-start.1
  106.8 7.7 slice-start.3
  114.5 6.0 copy-start.7
  159.0 15.3 %copy-start.4 = (bf16[2048,1024]{1,0:T(8,128)(2,1)S(1)}, bf16[2048,1024]{1,0:T(8,128)(2,1)}, u32[]{:S(2)}) copy-start(bf16[2048,1024]{1,0:T(8,128)(2,1)} %get-tuple-element.140) | copy-start | bytes 12582916 | tf_op jit(solution)/shard_map/cond
  159.0 15.3 %copy-start.5 = (bf16[1024,16,128]{0,2,1:T(8,128)(2,1)S(1)}, bf16[1024,16,128]{0,2,1:T(8,128)(2,1)}, u32[]{:S(2)}) copy-start(bf16[1024,16,128]{0,2,1:T(8,128)(2,1)} %copy.36) | copy-start | bytes 12582916 | tf_op jit(solution)/shard_map/cond
  729.9 10.7 %copy-start.3 = (bf16[128,32,128]{2,0,1:T(8,128)(2,1)S(1)}, bf16[128,32,128]{2,0,1:T(8,128)(2,1)}, u32[]{:S(2)}) copy-start(bf16[128,32,128]{2,0,1:T(8,128)(2,1)} %all_to_all.29) | copy-start | bytes 3145732
  729.9 10.7 %copy-start.10 = (f32[128]{0:T(128)S(1)}, f32[128]{0:T(128)}, u32[]{:S(2)}) copy-start(f32[128]{0:T(128)} %param.16) | copy-start | bytes 1540
  740.6 21.0 %copy-start.6 = (bf16[128,4096]{1,0:T(8,128)(2,1)S(1)}, bf16[128,4096]{1,0:T(8,128)(2,1)}, u32[]{:S(2)}) copy-start(bf16[128,4096]{1,0:T(8,128)(2,1)} %param.11) | copy-start | bytes 3145732
  762.9 103.0 %all-gather.8.cloned.1.call-start = ((), (), s32[]{:S(2)}) async-start(), calls=%async_computation.4 | async-start | bytes 8650752 | tf_op jit(solution)/shard_map/all_gather | solution.py:164
Sparse Core Ops, SparseCore 0:
  32.7 47.5 all-gather.3
  763.0 47.5 all-gather.5
  812.9 52.9 all-gather.7
where the time goes:
time: 895 us; the launch traced here: 883 us
  other arithmetic  333 us (37%)
  local copies, waits for them, and re-layouts  292 us (33%)
  waiting for transfers between devices  103 us (12%)
  matrix products  95.3 us (11%)
  blocking collectives  44.8 us (5%)
  between operations  13.5 us (2%)
    sub x16, other arithmetic, packed_product(): real_out = left_real * right_real - inner_mask * left_imag * right_imag  149 us
    slice x16, local copies, waits for them, and re-layouts, packed_product(): left_real, left_imag = (left_side[:block_len], left_side[block_len:])  140 us
    while x64, local copies, waits for them, and re-layouts  110 us
    add x16, other arithmetic, one_source(): return inner_sum + packed_product(window, source, block_len)  108 us
    all_gather x1, waiting for transfers between devices, on_device(): lax.all_gather(out_weight, 'chan', axis=0, tiled=True)  55.2 us
    all_gather x1, waiting for transfers between devices, on_device(): token_block = lax.all_gather(gated, 'seq', axis=0, tiled=True)  47 us
    mul x1, other arithmetic, inverse_matrix(): real_cols = scaling * jnp.cos(angles)  34.7 us
    dot_general x1, matrix products, lag_spectra(): jnp.einsum('kcm,rcm->krc', pole_terms, lag_weight, precision=precise)  31.7 us
  transfers between devices with their start and end apart: 3, of which 2 were waited for; matrix products, arithmetic and copies ran while one was open for 9% of the time, Pallas kernels for 0%

commit v1 on v0

v1 whole, which is shorter than its diff:
```python
import functools

import jax
import jax.numpy as jnp
from jax import lax
from jax.experimental import pallas as pl
from jax.experimental.pallas import tpu as pltpu
from jax.sharding import PartitionSpec as P

ORDER = 16
LANES = 128
ROWS = 8
UNROLL = 8
CHUNKS = 4
VMEM_LIMIT = 32 * 1024 * 1024


def states_kernel(rate_ref, key_ref, value_ref, signal_ref, state_ref):
    tokens = key_ref.shape[0]
    product = key_ref[...].astype(jnp.float32) * value_ref[...].astype(jnp.float32)
    product = product.astype(jnp.bfloat16).astype(jnp.float32)
    for j in range(ROWS):
        signal_ref[pl.ds(j, tokens, stride=ROWS), :] = product[:, j * LANES : (j + 1) * LANES]
    retain = [jnp.exp(-rate_ref[m]) for m in range(ORDER)]

    def several(step, held):
        for u in range(UNROLL):
            at = pl.multiple_of((step * UNROLL + u) * ROWS, ROWS)
            now = signal_ref[pl.ds(at, ROWS), :]
            held = [retain[m] * held[m] + now for m in range(ORDER)]
        return held

    zero = jnp.zeros((ROWS, LANES), jnp.float32)
    held = lax.fori_loop(0, tokens // UNROLL, several, [zero] * ORDER)
    for m in range(ORDER):
        state_ref[m] = held[m]


def tree_sum(terms):
    while len(terms) > 1:
        terms = [a + b for a, b in zip(terms[::2], terms[1::2])] + terms[len(terms) & ~1 :]
    return terms[0]


def local_kernel(param_ref, signal_ref, local_ref):
    tokens = signal_ref.shape[0] // ROWS
    retain = [jnp.exp(-param_ref[m]) for m in range(ORDER)]
    weight = [param_ref[ORDER + m] for m in range(ORDER)]
    skip = param_ref[2 * ORDER]

    def several(step, held):
        for u in range(UNROLL):
            at = pl.multiple_of((step * UNROLL + u) * ROWS, ROWS)
            now = signal_ref[pl.ds(at, ROWS), :]
            held = [retain[m] * held[m] + now for m in range(ORDER)]
            local_ref[pl.ds(at, ROWS), :] = (
                tree_sum([weight[m] * held[m] for m in range(ORDER)]) + skip * now
            )
        return held

    zero = jnp.zeros((ROWS, LANES), jnp.float32)
    lax.fori_loop(0, tokens // UNROLL, several, [zero] * ORDER)


def gate_kernel(param_ref, before_ref, local_ref, query_ref, gated_ref, mixed_ref):
    tokens = query_ref.shape[0]
    retain = [jnp.exp(-param_ref[m]) for m in range(ORDER)]
    start = [param_ref[ORDER + m] * before_ref[m] for m in range(ORDER)]

    def several(step, held):
        for u in range(UNROLL):
            at = pl.multiple_of((step * UNROLL + u) * ROWS, ROWS)
            held = [retain[m] * held[m] for m in range(ORDER)]
            mixed_ref[pl.ds(at, ROWS), :] = local_ref[pl.ds(at, ROWS), :] + tree_sum(held)
        return held

    lax.fori_loop(0, tokens // UNROLL, several, start)
    for j in range(ROWS):
        mixed = mixed_ref[pl.ds(j, tokens, stride=ROWS), :].astype(jnp.bfloat16)
        columns = slice(j * LANES, (j + 1) * LANES)
        gated = query_ref[:, columns].astype(jnp.float32) * mixed.astype(jnp.float32)
        gated_ref[:, columns] = gated.astype(jnp.bfloat16)


def compiler_params():
    return pltpu.CompilerParams(vmem_limit_bytes=VMEM_LIMIT)


def block_states(params, key_rows, value_rows):
    tokens, width = key_rows.shape
    groups = width // (ROWS * LANES)
    count = tokens * width * ORDER
    return pl.pallas_call(
        states_kernel,
        grid=(groups,),
        in_specs=[
            pl.BlockSpec((ORDER, ROWS, LANES), lambda g: (0, g, 0)),
            pl.BlockSpec((tokens, ROWS * LANES), lambda g: (0, g)),
            pl.BlockSpec((tokens, ROWS * LANES), lambda g: (0, g)),
        ],
        out_specs=[
            pl.BlockSpec((None, tokens * ROWS, LANES), lambda g: (g, 0, 0)),
            pl.BlockSpec((ORDER, ROWS, LANES), lambda g: (0, g, 0)),
        ],
        out_shape=[
            jax.ShapeDtypeStruct((groups, tokens * ROWS, LANES), jnp.float32),
            jax.ShapeDtypeStruct((ORDER, width // LANES, LANES), jnp.float32),
        ],
        compiler_params=compiler_params(),
        cost_estimate=pl.CostEstimate(flops=2 * count, bytes_accessed=8 * tokens * width, transcendentals=0),
        name="block_states",
    )(params, key_rows, value_rows)


def local_part(params, signal):
    groups, rows, _ = signal.shape
    count = groups * rows * LANES
    return pl.pallas_call(
        local_kernel,
        grid=(groups,),
        in_specs=[
            pl.BlockSpec((2 * ORDER + 1, ROWS, LANES), lambda g: (0, g, 0)),
            pl.BlockSpec((None, rows, LANES), lambda g: (g, 0, 0)),
        ],
        out_specs=pl.BlockSpec((None, rows, LANES), lambda g: (g, 0, 0)),
        out_shape=jax.ShapeDtypeStruct(signal.shape, jnp.float32),
        compiler_params=compiler_params(),
        cost_estimate=pl.CostEstimate(flops=4 * ORDER * count, bytes_accessed=8 * count, transcendentals=0),
        name="local_part",
    )(params, signal)


def gate_part(params, before, local, query_rows, first, count):
    tokens = query_rows.shape[0]
    size = tokens * ROWS * LANES * count
    return pl.pallas_call(
        gate_kernel,
        grid=(count,),
        in_specs=[
            pl.BlockSpec((2 * ORDER + 1, ROWS, LANES), lambda g: (0, g + first, 0)),
            pl.BlockSpec((ORDER, ROWS, LANES), lambda g: (0, g + first, 0)),
            pl.BlockSpec((None, tokens * ROWS, LANES), lambda g: (g + first, 0, 0)),
            pl.BlockSpec((tokens, ROWS * LANES), lambda g: (0, g + first)),
        ],
        out_specs=pl.BlockSpec((tokens, ROWS * LANES), lambda g: (0, g)),
        out_shape=jax.ShapeDtypeStruct((tokens, ROWS * LANES * count), jnp.bfloat16),
        scratch_shapes=[pltpu.VMEM((tokens * ROWS, LANES), jnp.float32)],
        compiler_params=compiler_params(),
        cost_estimate=pl.CostEstimate(flops=2 * ORDER * size, bytes_accessed=8 * size, transcendentals=0),
        name="gate_part",
    )(params, before, local, query_rows)


def combine(own, received, place, members, rate, span):
    position = place.astype(jnp.float32)
    decay = rate * float(span)
    total = jnp.exp(-decay * (members - 1 - position)) * own
    prefix = jnp.zeros_like(own)
    for s, other in enumerate(received, 1):
        other = other.astype(jnp.float32)
        earlier = place >= s
        power = jnp.where(earlier, members - 1 - position + s, s - 1 - position)
        total = total + jnp.exp(-decay * power) * other
        prefix = prefix + jnp.where(earlier, jnp.exp(-decay * (s - 1.0)) * other, 0.0)
    return total, prefix


def on_device(query_rows, key_rows, value_rows, residue, pole_rate, skip_gain, out_weight):
    tokens, width = query_rows.shape
    seq_count = lax.axis_size("seq")
    chan_count = lax.axis_size("chan")
    z, chan = lax.axis_index("seq"), lax.axis_index("chan")
    core, y, x = chan % 2, chan // 2 % 4, chan // 8
    length = tokens * seq_count * chan_count

    rate = pole_rate / length
    weight = residue * jnp.sqrt(2.0 * rate)
    own_params = jnp.concatenate([rate.T, weight.T, skip_gain[None, :]], axis=0)
    params = lax.all_gather(own_params, "chan", axis=1)
    full_weight = lax.all_gather(out_weight, "chan", axis=0, tiled=True)

    signal, state = block_states(params, key_rows, value_rows)
    local = local_part(params, signal)
    rates = params[:ORDER]

    def from_chan(array, shift):
        return lax.ppermute(array, "chan", [(i, shift(i)) for i in range(chan_count)])

    sent = state.astype(jnp.bfloat16)
    got = [from_chan(sent, lambda i: i ^ 1)]
    total, before = combine(state, got, core, 2, rates, tokens)

    sent = total.astype(jnp.bfloat16)
    got = [from_chan(sent, lambda i, s=s: i // 8 * 8 + (i + 2 * s) % 8) for s in (1, 2, 3)]
    total, prefix = combine(total, got, y, 4, rates, 2 * tokens)
    gone = (core * tokens).astype(jnp.float32)
    before = before + jnp.exp(-rates * gone) * prefix

    sent = total.astype(jnp.bfloat16)
    got = [from_chan(sent, lambda i, s=s: (i + 8 * s) % 32) for s in (1, 2, 3)]
    total, prefix = combine(total, got, x, 4, rates, 8 * tokens)
    gone = gone + (y * 2 * tokens).astype(jnp.float32)
    before = before + jnp.exp(-rates * gone) * prefix

    def from_seq(array, s):
        return lax.ppermute(array, "seq", [(i, (i + s) % seq_count) for i in range(seq_count)])

    sent = total.astype(jnp.bfloat16)
    got = [from_seq(sent, s) for s in (1, 2, 3)]
    _, prefix = combine(total, got, z, 4, rates, 32 * tokens)
    gone = gone + (x * 8 * tokens).astype(jnp.float32)
    before = before + jnp.exp(-rates * gone) * prefix

    groups = width // (ROWS * LANES)
    each = groups // CHUNKS
    half = tokens // 2
    sums = [None] * 4
    for c in range(CHUNKS):
        gated = gate_part(params, before, local, query_rows, c * each, each)
        rows = full_weight[c * each * ROWS * LANES : (c + 1) * each * ROWS * LANES]
        lower, upper = from_seq(gated, 1), from_seq(gated, -1)
        far_upper = from_seq(upper[half:], -1)
        far_lower = from_seq(lower[:half], 1)
        far = jnp.concatenate([far_lower, far_upper], axis=0)
        for n, part in enumerate((gated, upper, far, lower)):
            term = jnp.dot(part, rows, preferred_element_type=jnp.float32)
            sums[n] = term if sums[n] is None else sums[n] + term
    stacked = jnp.stack([s.astype(jnp.bfloat16) for s in sums])
    return jnp.roll(stacked, z, axis=0)


def solution(mesh):
    in_specs = (
        P(("seq", "chan"), None),
        P(("seq", "chan"), None),
        P(("seq", "chan"), None),
        P("chan", None),
        P("chan", None),
        P("chan"),
        P("chan", "seq"),
    )
    out_specs = P(None, "chan", "seq")
    return jax.shard_map(
        on_device, mesh=mesh, in_specs=in_specs, out_specs=out_specs, check_vma=False
    )
```

time: 895 us -> 160 us (0.18); the launches traced: 883 us -> 160 us
  other arithmetic: 333 us -> 9.1 us
  local copies, waits for them, and re-layouts: 292 us -> 16 us
  waiting for transfers between devices: 103 us -> 24.9 us
  matrix products: 95.3 us -> 17.5 us
  starting transfers between devices: 0.09 us -> 40 us
  blocking collectives: 44.8 us -> 26.7 us
  Pallas kernels: 0 us -> 11.2 us
    slice x32 -> x8, local copies, waits for them, and re-layouts: 160 us -> 5.25 us  [the longest x4 2.75 us: on_device(): far_lower = from_seq(lower[:half], 1)]
    sub x32 -> x0, other arithmetic: 149 us -> none  [the longest x16 149 us: packed_product(): real_out = left_real * right_real - inner_mask * left_imag * right_imag]
    while x64 -> x0, local copies, waits for them, and re-layouts: 110 us -> none
    add x17 -> x1, other arithmetic: 108 us -> 1.72 us  [on_device(): before = before + jnp.exp(-rates * gone) * prefix]
    all_gather x3 -> x1, waiting for transfers between devices: 102 us -> 0.02 us  [on_device(): full_weight = lax.all_gather(out_weight, 'chan', axis=0, tiled=True)]
    dot_general x6 -> x16, matrix products: 95.3 us -> 17.5 us  [on_device(): term = jnp.dot(part, rows, preferred_element_type=jnp.float32)]
    all_to_all x2 -> x0, blocking collectives: 44.8 us -> none  [the longest x1 24.1 us: on_device(): lax.all_to_all(product, 'chan', split_axis=1, concat_axis=0, tiled=True)]
    ppermute x0 -> x26, starting transfers between devices: none -> 40 us  [the longest x19 31.1 us: from_seq(): lax.ppermute(array, 'seq', [(i, (i + s) % seq_count) for i in range(seq_c...]
  transfers between devices with their start and end apart: 3 -> 27, of which waited for: 2 -> 5; matrix products, arithmetic and copies ran while one was open for 9% -> 24% of each run, Pallas kernels for 0% -> 7%
where the time goes in v1:
time: 160 us
  starting transfers between devices  40 us (25%)
  blocking collectives  26.7 us (17%)
  waiting for transfers between devices  24.9 us (16%)
  matrix products  17.5 us (11%)
  local copies, waits for them, and re-layouts  16 us (10%)
  between operations  14.3 us (9%)
  Pallas kernels  11.2 us (7%)
  other arithmetic  9.1 us (6%)
    ppermute x19, starting transfers between devices, from_seq(): lax.ppermute(array, 'seq', [(i, (i + s) % seq_count) for i in range(seq_c...  31.1 us
    all_gather x1, blocking collectives, on_device(): params = lax.all_gather(own_params, 'chan', axis=1)  26.7 us
    ppermute x7, waiting for transfers between devices, from_chan(): lax.ppermute(array, 'chan', [(i, shift(i)) for i in range(chan_count)])  17.9 us
    dot_general x16, matrix products, on_device(): term = jnp.dot(part, rows, preferred_element_type=jnp.float32)  17.5 us
    unnamed x97, local copies, waits for them, and re-layouts  9.68 us
    ppermute x7, starting transfers between devices, from_chan(): lax.ppermute(array, 'chan', [(i, shift(i)) for i in range(chan_count)])  8.93 us
    ppermute x19, waiting for transfers between devices, from_seq(): lax.ppermute(array, 'seq', [(i, (i + s) % seq_count) for i in range(seq_c...  6.32 us
    pallas_call x1, Pallas kernels, local_part(): pl.pallas_call(local_kernel, grid=(groups,), in_specs=[pl.BlockSpec((2 *...  4.88 us
  transfers between devices with their start and end apart: 27, of which 5 were waited for; matrix products, arithmetic and copies ran while one was open for 24% of the time, Pallas kernels for 7%

profile of v1, /device:TPU:0, one launch (start us, length us, event | category | flops | bytes accessed | tf_op | source)
XLA Modules:
  0.0 159.8 jit_solution(7193916024580539102)
XLA Ops:
  8.8 26.7 %all-gather = f32[33,4096]{1,0:T(8,128)S(1)} all-gather(f32[33,128]{1,0:T(8,128)S(1)} %pad_maximum_fusion), channel_id=2, replica_groups=mesh['seq'=4,'chan'=32] {'chan'}, dimensions={1}, use_global_device_ids=true | all-gather | bytes 557568 | tf_op jit(solution)/shard_map/all_gather | solution.py:179
  35.7 3.2 %block_states.1 = (f32[4,1024,128]{2,1,0:T(8,128)S(1)}, f32[16,32,128]{2,1,0:T(8,128)S(1)}) custom-call(f32[33,32,128]{2,1,0:T(8,128)S(1)} %slice.66.rate_ref.param_ref, bf16[128,4096]{1,0:T(8,128)(2,1)S(1)} %copy-done.1, bf16[128,4096]{1,0:T(8,128)(2,1)S(1)} %copy-done.2), custom_call_target="tpu_custom_call" | custom-call | flops 16777216 | bytes 4194304 | tf_op jit(solution)/shard_map/block_states/pallas_call | solution.py:93
  43.2 1.8 %copy.12 = f32[2,8,32,128]{3,2,1,0:T(8,128)} copy(f32[2,8,32,128]{3,1,2,0:T(8,128)} %get-tuple-element.32) | data formatting | bytes 524288
  47.4 3.1 %collective-permute-start.2 = (bf16[16,32,128]{2,1,0:T(8,128)(2,1)S(1)}, bf16[16,32,128]{2,1,0:T(8,128)(2,1)S(1)}, u32[]{:S(2)}, u32[]{:S(2)}) collective-permute-start(bf16[16,32,128]{2,1,0:T(8,128)(2,1)S(1)} %get-tuple-element.11), channel_id=1, source_target_pairs={{0,4},{1,5},{2,6},{3,7},{4,0},{5,1},{6,2},{7,3},{8,12},{9,13},{10,... | collective-permute-start | bytes 393224 | tf_op jit(solution)/shard_map/ppermute | solution.py:187
  52.2 4.1 %collective-permute-done.1 = bf16[16,32,128]{2,1,0:T(8,128)(2,1)S(1)} collective-permute-done((bf16[16,32,128]{2,1,0:T(8,128)(2,1)S(1)}, bf16[16,32,128]{2,1,0:T(8,128)(2,1)S(1)}, u32[]{:S(2)}, u32[]{:S(2)}) %collective-permute-start.1) | collective-permute-done | bytes 131104 | tf_op jit(solution)/shard_map/ppermute | solution.py:187
  56.3 6.7 %collective-permute-done.2 = bf16[16,32,128]{2,1,0:T(8,128)(2,1)S(1)} collective-permute-done((bf16[16,32,128]{2,1,0:T(8,128)(2,1)S(1)}, bf16[16,32,128]{2,1,0:T(8,128)(2,1)S(1)}, u32[]{:S(2)}, u32[]{:S(2)}) %collective-permute-start.2) | collective-permute-done | bytes 131104 | tf_op jit(solution)/shard_map/ppermute | solution.py:187
  63.2 2.7 %collective-permute-start.5 = (bf16[16,32,128]{2,1,0:T(8,128)(2,1)S(1)}, bf16[16,32,128]{2,1,0:T(8,128)(2,1)S(1)}, u32[]{:S(2)}, u32[]{:S(2)}) collective-permute-start(bf16[16,32,128]{2,1,0:T(8,128)(2,1)S(1)} %get-tuple-element.9), channel_id=1, source_target_pairs={{0,16},{1,17},{2,18},{3,19},{4,20},{5,21},{6,22},{7,23},{8,24},{9,... | collective-permute-start | bytes 393224 | tf_op jit(solution)/shard_map/ppermute | solution.py:187
  67.7 7.1 %collective-permute-done.4 = bf16[16,32,128]{2,1,0:T(8,128)(2,1)S(1)} collective-permute-done((bf16[16,32,128]{2,1,0:T(8,128)(2,1)S(1)}, bf16[16,32,128]{2,1,0:T(8,128)(2,1)S(1)}, u32[]{:S(2)}, u32[]{:S(2)}) %collective-permute-start.4) | collective-permute-done | bytes 131104 | tf_op jit(solution)/shard_map/ppermute | solution.py:187
  75.6 3.0 %collective-permute-start.9 = (bf16[16,32,128]{2,1,0:T(8,128)(2,1)}, bf16[16,32,128]{2,1,0:T(8,128)(2,1)}, u32[]{:S(2)}, u32[]{:S(2)}) collective-permute-start(bf16[16,32,128]{2,1,0:T(8,128)(2,1)} %fusion.113), channel_id=1, source_target_pairs={{0,96},{32,0},{64,32},{96,64},{1,97},{33,1},{65,33},{97,65},{2,98}... | collective-permute-start | bytes 393224 | tf_op jit(solution)/shard_map/ppermute | solution.py:206
  83.6 4.9 %local_part.1.local_ref = f32[4,1024,128]{2,1,0:T(8,128)S(1)} custom-call(f32[33,32,128]{2,1,0:T(8,128)S(1)} %slice.66.rate_ref.param_ref, f32[4,1024,128]{2,1,0:T(8,128)S(1)} %get-tuple-element.8.signal_ref), custom_call_target="tpu_custom_call" | custom-call | flops 33554432 | bytes 4194304 | tf_op jit(solution)/shard_map/local_part/pallas_call | solution.py:118
  91.1 2.4 %collective-permute-start.13 = (bf16[128,1024]{1,0:T(8,128)(2,1)S(1)}, bf16[128,1024]{1,0:T(8,128)(2,1)S(1)}, u32[]{:S(2)}, u32[]{:S(2)}) collective-permute-start(bf16[128,1024]{1,0:T(8,128)(2,1)S(1)} %gate_part.7), channel_id=1, source_target_pairs={{0,96},{32,0},{64,32},{96,64},{1,97},{33,1},{65,33},{97,65},{2,98}... | collective-permute-start | bytes 786440 | tf_op jit(solution)/shard_map/ppermute | solution.py:206
  94.5 1.8 %collective-permute-start.23 = (bf16[128,1024]{1,0:T(8,128)(2,1)S(1)}, bf16[128,1024]{1,0:T(8,128)(2,1)S(1)}, u32[]{:S(2)}, u32[]{:S(2)}) collective-permute-start(bf16[128,1024]{1,0:T(8,128)(2,1)S(1)} %gate_part.7), channel_id=1, source_target_pairs={{0,32},{32,64},{64,96},{96,0},{1,33},{33,65},{65,97},{97,1},{2,34}... | collective-permute-start | bytes 786440 | tf_op jit(solution)/shard_map/ppermute | solution.py:206
  97.2 3.3 %collective-permute-start.11 = (bf16[128,1024]{1,0:T(8,128)(2,1)S(1)}, bf16[128,1024]{1,0:T(8,128)(2,1)}, u32[]{:S(2)}, u32[]{:S(2)}) collective-permute-start(bf16[128,1024]{1,0:T(8,128)(2,1)S(1)} %gate_part.5), channel_id=1, source_target_pairs={{0,96},{32,0},{64,32},{96,64},{1,97},{33,1},{65,33},{97,65},{2,98}... | collective-permute-start | bytes 786440 | tf_op jit(solution)/shard_map/ppermute | solution.py:206
  100.5 1.8 %collective-permute-start.17 = (bf16[128,1024]{1,0:T(8,128)(2,1)S(1)}, bf16[128,1024]{1,0:T(8,128)(2,1)S(1)}, u32[]{:S(2)}, u32[]{:S(2)}) collective-permute-start(bf16[128,1024]{1,0:T(8,128)(2,1)S(1)} %gate_part.5), channel_id=1, source_target_pairs={{0,32},{32,64},{64,96},{96,0},{1,33},{33,65},{65,97},{97,1},{2,34}... | collective-permute-start | bytes 786440 | tf_op jit(solution)/shard_map/ppermute | solution.py:206
  103.1 2.9 %collective-permute-done.12 = bf16[128,1024]{1,0:T(8,128)(2,1)S(1)} collective-permute-done((bf16[128,1024]{1,0:T(8,128)(2,1)S(1)}, bf16[128,1024]{1,0:T(8,128)(2,1)S(1)}, u32[]{:S(2)}, u32[]{:S(2)}) %collective-permute-start.12) | collective-permute-done | bytes 262176 | tf_op jit(solution)/shard_map/ppermute | solution.py:206
  106.0 3.5 %collective-permute-start.10 = (bf16[128,1024]{1,0:T(8,128)(2,1)S(1)}, bf16[128,1024]{1,0:T(8,128)(2,1)S(1)}, u32[]{:S(2)}, u32[]{:S(2)}) collective-permute-start(bf16[128,1024]{1,0:T(8,128)(2,1)S(1)} %gate_part.4), channel_id=1, source_target_pairs={{0,96},{32,0},{64,32},{96,64},{1,97},{33,1},{65,33},{97,65},{2,98}... | collective-permute-start | bytes 786440 | tf_op jit(solution)/shard_map/ppermute | solution.py:206
  112.8 3.3 %collective-permute-start.25 = (bf16[64,1024]{1,0:T(8,128)(2,1)}, bf16[64,1024]{1,0:T(8,128)(2,1)}, u32[]{:S(2)}, u32[]{:S(2)}) collective-permute-start(bf16[64,1024]{1,0:T(8,128)(2,1)} %slice.65), channel_id=1, source_target_pairs={{0,96},{32,0},{64,32},{96,64},{1,97},{33,1},{65,33},{97,65},{2,98}... | collective-permute-start | bytes 393224 | tf_op jit(solution)/shard_map/ppermute | solution.py:206
  118.8 3.2 %collective-permute-start.22 = (bf16[64,1024]{1,0:T(8,128)(2,1)S(1)}, bf16[64,1024]{1,0:T(8,128)(2,1)}, u32[]{:S(2)}, u32[]{:S(2)}) collective-permute-start(bf16[64,1024]{1,0:T(8,128)(2,1)S(1)} %slice.63), channel_id=1, source_target_pairs={{0,96},{32,0},{64,32},{96,64},{1,97},{33,1},{65,33},{97,65},{2,98}... | collective-permute-start | bytes 393224 | tf_op jit(solution)/shard_map/ppermute | solution.py:206
  123.0 3.3 %collective-permute-start.19 = (bf16[64,1024]{1,0:T(8,128)(2,1)S(1)}, bf16[64,1024]{1,0:T(8,128)(2,1)}, u32[]{:S(2)}, u32[]{:S(2)}) collective-permute-start(bf16[64,1024]{1,0:T(8,128)(2,1)S(1)} %slice.61), channel_id=1, source_target_pairs={{0,96},{32,0},{64,32},{96,64},{1,97},{33,1},{65,33},{97,65},{2,98}... | collective-permute-start | bytes 393224 | tf_op jit(solution)/shard_map/ppermute | solution.py:206
  126.3 2.2 %fusion.6 = f32[128,1024]{1,0:T(8,128)S(1)} fusion(bf16[128,1024]{1,0:T(8,128)(2,1)S(1)} %gate_part.7, bf16[4096,1024]{1,0:T(8,128)(2,1)} %all-gather.3.cloned.1.call-done), kind=kOutput, calls=%fused_computation.6 | convolution fusion | flops 268435456 | bytes 2883584 | tf_op jit(solution)/shard_map/dot_general | solution.py:226
  128.5 2.5 %fusion.14 = f32[128,1024]{1,0:T(8,128)S(1)} fusion(bf16[128,1024]{1,0:T(8,128)(2,1)S(1)} %gate_part.6, bf16[4096,1024]{1,0:T(8,128)(2,1)} %all-gather.3.cloned.1.call-done), kind=kOutput, calls=%fused_computation.14 | convolution fusion | flops 268435456 | bytes 2883584 | tf_op jit(solution)/shard_map/dot_general | solution.py:226
  131.0 2.1 %fusion.22 = f32[128,1024]{1,0:T(8,128)S(1)} fusion(bf16[128,1024]{1,0:T(8,128)(2,1)S(1)} %gate_part.5, bf16[4096,1024]{1,0:T(8,128)(2,1)} %all-gather.3.cloned.1.call-done), kind=kOutput, calls=%fused_computation.22 | convolution fusion | flops 268435456 | bytes 2883584 | tf_op jit(solution)/shard_map/dot_general | solution.py:226
  139.9 3.2 %collective-permute-start.16 = (bf16[64,1024]{1,0:T(8,128)(2,1)S(1)}, bf16[64,1024]{1,0:T(8,128)(2,1)S(1)}, u32[]{:S(2)}, u32[]{:S(2)}) collective-permute-start(bf16[64,1024]{1,0:T(8,128)(2,1)S(1)} %slice.59), channel_id=1, source_target_pairs={{0,96},{32,0},{64,32},{96,64},{1,97},{33,1},{65,33},{97,65},{2,98}... | collective-permute-start | bytes 393224 | tf_op jit(solution)/shard_map/ppermute | solution.py:206
  147.4 3.3 %collective-permute-done.15 = bf16[64,1024]{1,0:T(8,128)(2,1)S(1)} collective-permute-done((bf16[64,1024]{1,0:T(8,128)(2,1)S(1)}, bf16[64,1024]{1,0:T(8,128)(2,1)S(1)}, u32[]{:S(2)}, u32[]{:S(2)}) %collective-permute-start.15) | collective-permute-done | bytes 131104 | tf_op jit(solution)/shard_map/ppermute | solution.py:206
  (171 shorter events, 43.4 us)
Async XLA Ops:
  6.5 119.8 %all-gather.3.cloned.1.call-start = ((), (), s32[]{:S(2)}) async-start(), calls=%async_computation | async-start | bytes 8650752 | tf_op jit(solution)/shard_map/all_gather | solution.py:180
  46.1 10.2 %collective-permute-start.1 = (bf16[16,32,128]{2,1,0:T(8,128)(2,1)S(1)}, bf16[16,32,128]{2,1,0:T(8,128)(2,1)S(1)}, u32[]{:S(2)}, u32[]{:S(2)}) collective-permute-start(bf16[16,32,128]{2,1,0:T(8,128)(2,1)S(1)} %get-tuple-element.11), channel_id=1, source_target_pairs={{0,2},{1,3},{2,4},{3,5},{4,6},{5,7},{6,0},{7,1},{8,10},{9,11},{10,... | collective-permute-start | bytes 393224 | tf_op jit(solution)/shard_map/ppermute | solution.py:187
  47.4 15.6 %collective-permute-start.2 = (bf16[16,32,128]{2,1,0:T(8,128)(2,1)S(1)}, bf16[16,32,128]{2,1,0:T(8,128)(2,1)S(1)}, u32[]{:S(2)}, u32[]{:S(2)}) collective-permute-start(bf16[16,32,128]{2,1,0:T(8,128)(2,1)S(1)} %get-tuple-element.11), channel_id=1, source_target_pairs={{0,4},{1,5},{2,6},{3,7},{4,0},{5,1},{6,2},{7,3},{8,12},{9,13},{10,... | collective-permute-start | bytes 393224 | tf_op jit(solution)/shard_map/ppermute | solution.py:187
  50.5 12.5 %collective-permute-start.3 = (bf16[16,32,128]{2,1,0:T(8,128)(2,1)S(1)}, bf16[16,32,128]{2,1,0:T(8,128)(2,1)S(1)}, u32[]{:S(2)}, u32[]{:S(2)}) collective-permute-start(bf16[16,32,128]{2,1,0:T(8,128)(2,1)S(1)} %get-tuple-element.11), channel_id=1, source_target_pairs={{0,6},{1,7},{2,0},{3,1},{4,2},{5,3},{6,4},{7,5},{8,14},{9,15},{10,... | collective-permute-start | bytes 393224 | tf_op jit(solution)/shard_map/ppermute | solution.py:187
  63.1 11.7 %collective-permute-start.4 = (bf16[16,32,128]{2,1,0:T(8,128)(2,1)S(1)}, bf16[16,32,128]{2,1,0:T(8,128)(2,1)S(1)}, u32[]{:S(2)}, u32[]{:S(2)}) collective-permute-start(bf16[16,32,128]{2,1,0:T(8,128)(2,1)S(1)} %get-tuple-element.9), channel_id=1, source_target_pairs={{0,8},{1,9},{2,10},{3,11},{4,12},{5,13},{6,14},{7,15},{8,16},{9,17... | collective-permute-start | bytes 393224 | tf_op jit(solution)/shard_map/ppermute | solution.py:187
  63.2 11.6 %collective-permute-start.5 = (bf16[16,32,128]{2,1,0:T(8,128)(2,1)S(1)}, bf16[16,32,128]{2,1,0:T(8,128)(2,1)S(1)}, u32[]{:S(2)}, u32[]{:S(2)}) collective-permute-start(bf16[16,32,128]{2,1,0:T(8,128)(2,1)S(1)} %get-tuple-element.9), channel_id=1, source_target_pairs={{0,16},{1,17},{2,18},{3,19},{4,20},{5,21},{6,22},{7,23},{8,24},{9,... | collective-permute-start | bytes 393224 | tf_op jit(solution)/shard_map/ppermute | solution.py:187
  65.9 8.9 %collective-permute-start.6 = (bf16[16,32,128]{2,1,0:T(8,128)(2,1)S(1)}, bf16[16,32,128]{2,1,0:T(8,128)(2,1)S(1)}, u32[]{:S(2)}, u32[]{:S(2)}) collective-permute-start(bf16[16,32,128]{2,1,0:T(8,128)(2,1)S(1)} %get-tuple-element.9), channel_id=1, source_target_pairs={{0,24},{1,25},{2,26},{3,27},{4,28},{5,29},{6,30},{7,31},{8,0},{9,1... | collective-permute-start | bytes 393224 | tf_op jit(solution)/shard_map/ppermute | solution.py:187
  75.6 12.9 %collective-permute-start.9 = (bf16[16,32,128]{2,1,0:T(8,128)(2,1)}, bf16[16,32,128]{2,1,0:T(8,128)(2,1)}, u32[]{:S(2)}, u32[]{:S(2)}) collective-permute-start(bf16[16,32,128]{2,1,0:T(8,128)(2,1)} %fusion.113), channel_id=1, source_target_pairs={{0,96},{32,0},{64,32},{96,64},{1,97},{33,1},{65,33},{97,65},{2,98}... | collective-permute-start | bytes 393224 | tf_op jit(solution)/shard_map/ppermute | solution.py:206
  78.6 9.9 %collective-permute-start.8 = (bf16[16,32,128]{2,1,0:T(8,128)(2,1)}, bf16[16,32,128]{2,1,0:T(8,128)(2,1)}, u32[]{:S(2)}, u32[]{:S(2)}) collective-permute-start(bf16[16,32,128]{2,1,0:T(8,128)(2,1)} %fusion.113), channel_id=1, source_target_pairs={{0,64},{32,96},{64,0},{96,32},{1,65},{33,97},{65,1},{97,33},{2,66}... | collective-permute-start | bytes 393224 | tf_op jit(solution)/shard_map/ppermute | solution.py:206
  79.3 9.2 %collective-permute-start.7 = (bf16[16,32,128]{2,1,0:T(8,128)(2,1)}, bf16[16,32,128]{2,1,0:T(8,128)(2,1)}, u32[]{:S(2)}, u32[]{:S(2)}) collective-permute-start(bf16[16,32,128]{2,1,0:T(8,128)(2,1)} %fusion.113), channel_id=1, source_target_pairs={{0,32},{32,64},{64,96},{96,0},{1,33},{33,65},{65,97},{97,1},{2,34}... | collective-permute-start | bytes 393224 | tf_op jit(solution)/shard_map/ppermute | solution.py:206
  91.1 9.4 %collective-permute-start.13 = (bf16[128,1024]{1,0:T(8,128)(2,1)S(1)}, bf16[128,1024]{1,0:T(8,128)(2,1)S(1)}, u32[]{:S(2)}, u32[]{:S(2)}) collective-permute-start(bf16[128,1024]{1,0:T(8,128)(2,1)S(1)} %gate_part.7), channel_id=1, source_target_pairs={{0,96},{32,0},{64,32},{96,64},{1,97},{33,1},{65,33},{97,65},{2,98}... | collective-permute-start | bytes 786440 | tf_op jit(solution)/shard_map/ppermute | solution.py:206
  94.3 11.7 %collective-permute-start.12 = (bf16[128,1024]{1,0:T(8,128)(2,1)S(1)}, bf16[128,1024]{1,0:T(8,128)(2,1)S(1)}, u32[]{:S(2)}, u32[]{:S(2)}) collective-permute-start(bf16[128,1024]{1,0:T(8,128)(2,1)S(1)} %gate_part.6), channel_id=1, source_target_pairs={{0,96},{32,0},{64,32},{96,64},{1,97},{33,1},{65,33},{97,65},{2,98}... | collective-permute-start | bytes 786440 | tf_op jit(solution)/shard_map/ppermute | solution.py:206
  94.5 15.0 %collective-permute-start.23 = (bf16[128,1024]{1,0:T(8,128)(2,1)S(1)}, bf16[128,1024]{1,0:T(8,128)(2,1)S(1)}, u32[]{:S(2)}, u32[]{:S(2)}) collective-permute-start(bf16[128,1024]{1,0:T(8,128)(2,1)S(1)} %gate_part.7), channel_id=1, source_target_pairs={{0,32},{32,64},{64,96},{96,0},{1,33},{33,65},{65,97},{97,1},{2,34}... | collective-permute-start | bytes 786440 | tf_op jit(solution)/shard_map/ppermute | solution.py:206
  96.4 16.4 %collective-permute-start.20 = (bf16[128,1024]{1,0:T(8,128)(2,1)S(1)}, bf16[128,1024]{1,0:T(8,128)(2,1)}, u32[]{:S(2)}, u32[]{:S(2)}) collective-permute-start(bf16[128,1024]{1,0:T(8,128)(2,1)S(1)} %gate_part.6), channel_id=1, source_target_pairs={{0,32},{32,64},{64,96},{96,0},{1,33},{33,65},{65,97},{97,1},{2,34}... | collective-permute-start | bytes 786440 | tf_op jit(solution)/shard_map/ppermute | solution.py:206
  97.2 19.8 %collective-permute-start.11 = (bf16[128,1024]{1,0:T(8,128)(2,1)S(1)}, bf16[128,1024]{1,0:T(8,128)(2,1)}, u32[]{:S(2)}, u32[]{:S(2)}) collective-permute-start(bf16[128,1024]{1,0:T(8,128)(2,1)S(1)} %gate_part.5), channel_id=1, source_target_pairs={{0,96},{32,0},{64,32},{96,64},{1,97},{33,1},{65,33},{97,65},{2,98}... | collective-permute-start | bytes 786440 | tf_op jit(solution)/shard_map/ppermute | solution.py:206
  100.5 17.6 %collective-permute-start.17 = (bf16[128,1024]{1,0:T(8,128)(2,1)S(1)}, bf16[128,1024]{1,0:T(8,128)(2,1)S(1)}, u32[]{:S(2)}, u32[]{:S(2)}) collective-permute-start(bf16[128,1024]{1,0:T(8,128)(2,1)S(1)} %gate_part.5), channel_id=1, source_target_pairs={{0,32},{32,64},{64,96},{96,0},{1,33},{33,65},{65,97},{97,1},{2,34}... | collective-permute-start | bytes 786440 | tf_op jit(solution)/shard_map/ppermute | solution.py:206
  106.0 16.9 %collective-permute-start.10 = (bf16[128,1024]{1,0:T(8,128)(2,1)S(1)}, bf16[128,1024]{1,0:T(8,128)(2,1)S(1)}, u32[]{:S(2)}, u32[]{:S(2)}) collective-permute-start(bf16[128,1024]{1,0:T(8,128)(2,1)S(1)} %gate_part.4), channel_id=1, source_target_pairs={{0,96},{32,0},{64,32},{96,64},{1,97},{33,1},{65,33},{97,65},{2,98}... | collective-permute-start | bytes 786440 | tf_op jit(solution)/shard_map/ppermute | solution.py:206
  110.3 12.7 %collective-permute-start.14 = (bf16[128,1024]{1,0:T(8,128)(2,1)S(1)}, bf16[128,1024]{1,0:T(8,128)(2,1)S(1)}, u32[]{:S(2)}, u32[]{:S(2)}) collective-permute-start(bf16[128,1024]{1,0:T(8,128)(2,1)S(1)} %gate_part.4), channel_id=1, source_target_pairs={{0,32},{32,64},{64,96},{96,0},{1,33},{33,65},{65,97},{97,1},{2,34}... | collective-permute-start | bytes 786440 | tf_op jit(solution)/shard_map/ppermute | solution.py:206
  112.8 27.0 %collective-permute-start.25 = (bf16[64,1024]{1,0:T(8,128)(2,1)}, bf16[64,1024]{1,0:T(8,128)(2,1)}, u32[]{:S(2)}, u32[]{:S(2)}) collective-permute-start(bf16[64,1024]{1,0:T(8,128)(2,1)} %slice.65), channel_id=1, source_target_pairs={{0,96},{32,0},{64,32},{96,64},{1,97},{33,1},{65,33},{97,65},{2,98}... | collective-permute-start | bytes 393224 | tf_op jit(solution)/shard_map/ppermute | solution.py:206
  117.0 22.8 %collective-permute-start.24 = (bf16[64,1024]{1,0:T(8,128)(2,1)S(1)}, bf16[64,1024]{1,0:T(8,128)(2,1)}, u32[]{:S(2)}, u32[]{:S(2)}) collective-permute-start(bf16[64,1024]{1,0:T(8,128)(2,1)S(1)} %slice.64), channel_id=1, source_target_pairs={{0,32},{32,64},{64,96},{96,0},{1,33},{33,65},{65,97},{97,1},{2,34}... | collective-permute-start | bytes 393224 | tf_op jit(solution)/shard_map/ppermute | solution.py:206
  118.8 25.8 %collective-permute-start.22 = (bf16[64,1024]{1,0:T(8,128)(2,1)S(1)}, bf16[64,1024]{1,0:T(8,128)(2,1)}, u32[]{:S(2)}, u32[]{:S(2)}) collective-permute-start(bf16[64,1024]{1,0:T(8,128)(2,1)S(1)} %slice.63), channel_id=1, source_target_pairs={{0,96},{32,0},{64,32},{96,64},{1,97},{33,1},{65,33},{97,65},{2,98}... | collective-permute-start | bytes 393224 | tf_op jit(solution)/shard_map/ppermute | solution.py:206
  122.9 21.7 %collective-permute-start.21 = (bf16[64,1024]{1,0:T(8,128)(2,1)S(1)}, bf16[64,1024]{1,0:T(8,128)(2,1)}, u32[]{:S(2)}, u32[]{:S(2)}) collective-permute-start(bf16[64,1024]{1,0:T(8,128)(2,1)S(1)} %slice.62), channel_id=1, source_target_pairs={{0,32},{32,64},{64,96},{96,0},{1,33},{33,65},{65,97},{97,1},{2,34}... | collective-permute-start | bytes 393224 | tf_op jit(solution)/shard_map/ppermute | solution.py:206
  123.0 23.0 %collective-permute-start.19 = (bf16[64,1024]{1,0:T(8,128)(2,1)S(1)}, bf16[64,1024]{1,0:T(8,128)(2,1)}, u32[]{:S(2)}, u32[]{:S(2)}) collective-permute-start(bf16[64,1024]{1,0:T(8,128)(2,1)S(1)} %slice.61), channel_id=1, source_target_pairs={{0,96},{32,0},{64,32},{96,64},{1,97},{33,1},{65,33},{97,65},{2,98}... | collective-permute-start | bytes 393224 | tf_op jit(solution)/shard_map/ppermute | solution.py:206
  139.9 7.5 %collective-permute-start.16 = (bf16[64,1024]{1,0:T(8,128)(2,1)S(1)}, bf16[64,1024]{1,0:T(8,128)(2,1)S(1)}, u32[]{:S(2)}, u32[]{:S(2)}) collective-permute-start(bf16[64,1024]{1,0:T(8,128)(2,1)S(1)} %slice.59), channel_id=1, source_target_pairs={{0,96},{32,0},{64,32},{96,64},{1,97},{33,1},{65,33},{97,65},{2,98}... | collective-permute-start | bytes 393224 | tf_op jit(solution)/shard_map/ppermute | solution.py:206
  (38 other events, 226.4 us)
Sparse Core Ops, SparseCore 0:
  9.6 64.4 all-gather.2

commit v2 on v0

v2 whole, which is shorter than its diff:
```python
import functools

import jax
import jax.numpy as jnp
from jax import lax
from jax.experimental import pallas as pl
from jax.experimental.pallas import tpu as pltpu
from jax.sharding import PartitionSpec as P

ORDER = 16
LANES = 128
ROWS = 8
GROUP = ROWS * LANES
UNROLL = 8
PARAMS = 5 * ORDER
SMALL_LIMIT = 16 * 1024 * 1024
LARGE_LIMIT = 56 * 1024 * 1024
COLUMNS = 256


def call(kernel, name, limit=SMALL_LIMIT, **keywords):
    return pl.pallas_call(
        kernel,
        name=name,
        compiler_params=pltpu.CompilerParams(vmem_limit_bytes=limit),
        cost_estimate=pl.CostEstimate(flops=1024, bytes_accessed=1024, transcendentals=0),
        **keywords,
    )


def as_float(block):
    return block.astype(jnp.float32)


def tree_sum(terms):
    while len(terms) > 1:
        terms = [a + b for a, b in zip(terms[::2], terms[1::2])] + terms[len(terms) & ~1 :]
    return terms[0]


def over_tokens(tokens, step, held):
    def several(outer, held):
        for u in range(UNROLL):
            held = step(pl.multiple_of((outer * UNROLL + u) * ROWS, ROWS), held)
        return held

    return lax.fori_loop(0, tokens // UNROLL, several, held)


def signal_kernel(key_ref, value_ref, signal_ref):
    signal = (as_float(key_ref[...]) * as_float(value_ref[...])).astype(jnp.bfloat16)
    for j in range(ROWS):
        signal_ref[j] = signal[:, j * LANES : (j + 1) * LANES]


def make_signal(key_rows, value_rows):
    tokens, width = key_rows.shape
    natural = pl.BlockSpec((tokens, GROUP), lambda g: (0, g))
    return call(
        signal_kernel,
        "signal",
        limit=LARGE_LIMIT,
        grid=(width // GROUP,),
        in_specs=[natural, natural],
        out_specs=pl.BlockSpec((ROWS, tokens, LANES), lambda g: (g, 0, 0)),
        out_shape=jax.ShapeDtypeStruct((width // LANES, tokens, LANES), jnp.bfloat16),
    )(key_rows, value_rows)


def states_kernel(tokens, rate_ref, signal_ref, prefix_ref, total_ref, work_ref, state_ref):
    for j in range(ROWS):
        work_ref[pl.ds(j, tokens, stride=ROWS), :] = as_float(signal_ref[j])
    rate = rate_ref[...]
    retain = [
        jnp.broadcast_to(jnp.exp(-rate[m : m + 1, :]), (ROWS, LANES)) for m in range(ORDER)
    ]

    def step(at, held):
        now = work_ref[pl.ds(at, ROWS), :]
        return [retain[m] * held[m] + now for m in range(ORDER)]

    held = over_tokens(tokens, step, [jnp.zeros((ROWS, LANES), jnp.float32)] * ORDER)
    for m in range(ORDER):
        state_ref[pl.ds(m, ROWS, stride=ORDER), :] = held[m]

    @pl.when(pl.program_id(0) == 0)
    def _():
        total_ref[...] = jnp.zeros_like(total_ref)

    decay = jnp.exp(-rate * float(tokens))
    before = total_ref[...]
    for j in range(ROWS):
        prefix_ref[j * ORDER : (j + 1) * ORDER, :] = before
        before = decay * before + state_ref[j * ORDER : (j + 1) * ORDER, :]
    total_ref[...] = before


def block_states(tokens, rate, received):
    blocks, _, lanes = received.shape
    return call(
        functools.partial(states_kernel, tokens),
        "block_states",
        grid=(blocks // ROWS,),
        in_specs=[
            pl.BlockSpec((ORDER, lanes), lambda g: (0, 0)),
            pl.BlockSpec((ROWS, tokens, lanes), lambda g: (g, 0, 0)),
        ],
        out_specs=[
            pl.BlockSpec((ROWS * ORDER, lanes), lambda g: (g, 0)),
            pl.BlockSpec((ORDER, lanes), lambda g: (0, 0)),
        ],
        out_shape=[
            jax.ShapeDtypeStruct((blocks * ORDER, lanes), jnp.float32),
            jax.ShapeDtypeStruct((ORDER, lanes), jnp.float32),
        ],
        scratch_shapes=[
            pltpu.VMEM((tokens * ROWS, lanes), jnp.float32),
            pltpu.VMEM((ROWS * ORDER, lanes), jnp.float32),
        ],
    )(rate, received)


def before_kernel(tokens, place_ref, rate_ref, weight_ref, skip_ref, prefix_ref, *refs):
    *total_refs, packed_ref = refs
    blocks = packed_ref.shape[0]
    rate = rate_ref[...]

    def pair(value):
        high = value.astype(jnp.bfloat16)
        return [high, (value - as_float(high)).astype(jnp.bfloat16)]

    skip = [as_float(part) for part in pair(skip_ref[...])]
    index = lax.broadcasted_iota(jnp.int32, (ORDER, LANES), 0)
    skip = jnp.where(index == 0, skip[0], jnp.where(index == 1, skip[1], 0.0))
    params = pair(rate) + pair(weight_ref[...]) + [skip.astype(jnp.bfloat16)]
    decay = jnp.exp(-rate * float(tokens))
    start = jnp.zeros((ORDER, LANES), jnp.float32)
    for s, total_ref in enumerate(total_refs, 1):
        passed = jnp.exp(-rate * float(tokens * blocks * (s - 1)))
        start = start + jnp.where(place_ref[0] >= s, passed * total_ref[...], 0.0)
    for i in range(blocks):
        for n, part in enumerate(params):
            packed_ref[i, n * ORDER : (n + 1) * ORDER, :] = part
        before = prefix_ref[i * ORDER : (i + 1) * ORDER, :] + start
        packed_ref[i, PARAMS:, :] = before.astype(jnp.bfloat16)
        start = decay * start


def states_before(tokens, z, rate, weight, skip, prefix, totals):
    whole = pl.BlockSpec(memory_space=pltpu.VMEM)
    return call(
        functools.partial(before_kernel, tokens),
        "states_before",
        in_specs=[pl.BlockSpec(memory_space=pltpu.SMEM)] + [whole] * (4 + len(totals)),
        out_specs=whole,
        out_shape=jax.ShapeDtypeStruct(
            (prefix.shape[0] // ORDER, PARAMS + ORDER, LANES), jnp.bfloat16
        ),
    )(z.reshape(1), rate, weight, skip, prefix, *totals)


def gate_kernel(packed_ref, before_ref, signal_ref, query_ref, gated_ref, part_ref, start_ref, work_ref):
    tokens = query_ref.shape[0]
    for j in range(ROWS):
        part_ref[j * PARAMS : (j + 1) * PARAMS, :] = as_float(packed_ref[j])
        start_ref[j * ORDER : (j + 1) * ORDER, :] = as_float(before_ref[j])
        work_ref[pl.ds(j, tokens, stride=ROWS), :] = as_float(signal_ref[j])

    def row(n):
        return part_ref[pl.ds(n, ROWS, stride=PARAMS), :]

    retain = [jnp.exp(-(row(m) + row(ORDER + m))) for m in range(ORDER)]
    weight = [row(2 * ORDER + m) + row(3 * ORDER + m) for m in range(ORDER)]
    skip = row(4 * ORDER) + row(4 * ORDER + 1)
    start = [start_ref[pl.ds(m, ROWS, stride=ORDER), :] for m in range(ORDER)]

    def step(at, held):
        now = work_ref[pl.ds(at, ROWS), :]
        held = [retain[m] * held[m] + now for m in range(ORDER)]
        terms = [weight[m] * held[m] for m in range(ORDER)]
        work_ref[pl.ds(at, ROWS), :] = tree_sum(terms) + skip * now
        return held

    over_tokens(tokens, step, start)
    for j in range(ROWS):
        mixed = work_ref[pl.ds(j, tokens, stride=ROWS), :].astype(jnp.bfloat16)
        columns = slice(j * LANES, (j + 1) * LANES)
        gated = as_float(query_ref[:, columns]) * as_float(mixed)
        gated_ref[:, columns] = gated.astype(jnp.bfloat16)


def gate_rows(packed, before, signal, query, first, count):
    tokens = query.shape[0]
    last = before.shape[1] // ORDER - 1
    return call(
        gate_kernel,
        "gate_rows",
        grid=(count,),
        in_specs=[
            pl.BlockSpec((ROWS, PARAMS, LANES), lambda g: (g + first, 0, 0)),
            pl.BlockSpec((ROWS, ORDER, LANES), lambda g: (g + first, last, 0)),
            pl.BlockSpec((ROWS, tokens, LANES), lambda g: (g + first, 0, 0)),
            pl.BlockSpec((tokens, GROUP), lambda g: (0, g + first)),
        ],
        out_specs=pl.BlockSpec((tokens, GROUP), lambda g: (0, g)),
        out_shape=jax.ShapeDtypeStruct((tokens, GROUP * count), jnp.bfloat16),
        scratch_shapes=[
            pltpu.VMEM((ROWS * PARAMS, LANES), jnp.float32),
            pltpu.VMEM((ROWS * ORDER, LANES), jnp.float32),
            pltpu.VMEM((tokens * ROWS, LANES), jnp.float32),
        ],
    )(packed, before, signal, query)


def whole_kernel(first_ref, second_ref, far_ref, matrix_ref, out_ref, rows_ref):
    tokens, split = first_ref.shape
    rows_ref[:tokens, :split] = first_ref[...]
    rows_ref[:tokens, split:] = second_ref[...]
    rows_ref[tokens:, :] = far_ref[...]
    for n in range(0, out_ref.shape[1], COLUMNS):
        columns = slice(n, n + COLUMNS)
        product = jnp.dot(rows_ref[...], matrix_ref[:, columns], preferred_element_type=jnp.float32)
        out_ref[:, columns] = product.astype(jnp.bfloat16)


def whole_rows(first, second, far, matrix):
    whole = pl.BlockSpec(memory_space=pltpu.VMEM)
    tokens, columns = far.shape[0], matrix.shape[1]
    return call(
        whole_kernel,
        "whole_rows",
        in_specs=[whole] * 4,
        out_specs=whole,
        out_shape=jax.ShapeDtypeStruct((2 * tokens, columns), jnp.bfloat16),
        scratch_shapes=[pltpu.VMEM((2 * tokens, far.shape[1]), jnp.bfloat16)],
    )(first, second, far, matrix)


def half_kernel(upper_ref, lower_ref, matrix_ref, sum_ref, rows_ref):
    tokens, depth = upper_ref.shape
    rows_ref[:tokens, :] = upper_ref[...]
    rows_ref[tokens:, :] = lower_ref[...]
    for n in range(0, sum_ref.shape[1], COLUMNS):
        columns = slice(n, n + COLUMNS)
        sum_ref[:, columns] = jnp.dot(
            rows_ref[...], matrix_ref[:depth, columns], preferred_element_type=jnp.float32
        )


def half_rows(upper, lower, matrix):
    whole = pl.BlockSpec(memory_space=pltpu.VMEM)
    tokens, depth = upper.shape
    return call(
        half_kernel,
        "half_rows",
        in_specs=[whole] * 3,
        out_specs=whole,
        out_shape=jax.ShapeDtypeStruct((2 * tokens, matrix.shape[1]), jnp.float32),
        scratch_shapes=[pltpu.VMEM((2 * tokens, depth), jnp.bfloat16)],
    )(upper, lower, matrix)


def finish_kernel(place_ref, done_ref, sum_ref, upper_ref, lower_ref, matrix_ref, out_ref, rows_ref):
    tokens, depth = upper_ref.shape
    rows_ref[:tokens, :] = upper_ref[...]
    rows_ref[tokens:, :] = lower_ref[...]
    own, up, far, low = [lax.rem(place_ref[0] + r, 4) for r in range(4)]
    out_ref[own] = done_ref[:tokens, :]
    out_ref[far] = done_ref[tokens:, :]
    for n in range(0, out_ref.shape[2], COLUMNS):
        columns = slice(n, n + COLUMNS)
        matrix = matrix_ref[matrix_ref.shape[0] - depth :, columns]
        product = jnp.dot(rows_ref[...], matrix, preferred_element_type=jnp.float32)
        total = (sum_ref[:, columns] + product).astype(jnp.bfloat16)
        out_ref[up, :, columns] = total[:tokens]
        out_ref[low, :, columns] = total[tokens:]


def finish(z, done, early_sum, upper, lower, matrix):
    tokens, depth = upper.shape
    whole = pl.BlockSpec(memory_space=pltpu.VMEM)
    return call(
        finish_kernel,
        "finish",
        in_specs=[pl.BlockSpec(memory_space=pltpu.SMEM)] + [whole] * 5,
        out_specs=whole,
        out_shape=jax.ShapeDtypeStruct((4, tokens, matrix.shape[1]), jnp.bfloat16),
        scratch_shapes=[pltpu.VMEM((2 * tokens, depth), jnp.bfloat16)],
    )(z.reshape(1), done, early_sum, upper, lower, matrix)


def on_device(query_rows, key_rows, value_rows, residue, pole_rate, skip_gain, out_weight):
    tokens, width = query_rows.shape
    seq_count = lax.axis_size("seq")
    length = tokens * seq_count * lax.axis_size("chan")
    z = lax.axis_index("seq")
    half = width // GROUP // 2

    def from_seq(array, s):
        return lax.ppermute(array, "seq", [(i, (i + s) % seq_count) for i in range(seq_count)])

    def to_owners(array):
        return lax.all_to_all(array, "chan", split_axis=0, concat_axis=0, tiled=True)

    rate = pole_rate / length
    weight = (residue * jnp.sqrt(2.0 * rate)).T
    rate = rate.T
    far_query = from_seq(query_rows, 2)
    signal = make_signal(key_rows, value_rows)
    received = to_owners(signal)
    received, far_query, out_weight = lax.optimization_barrier((received, far_query, out_weight))
    full_weight = lax.all_gather(out_weight, "chan", axis=0, tiled=True)

    prefix, total = block_states(tokens, rate, received)
    totals = [from_seq(total, s) for s in (1, 2, 3)]
    packed = states_before(tokens, z, rate, weight, skip_gain[None, :], prefix, totals)
    packed, signal = lax.optimization_barrier((packed, signal))
    far_signal = from_seq(signal, 2)
    packed = to_owners(packed)
    packed, far_signal = lax.optimization_barrier((packed, far_signal))

    far_before = from_seq(packed[:, PARAMS:], 2)
    first = gate_rows(packed, packed, signal, query_rows, 0, half)
    first, far_before = lax.optimization_barrier((first, far_before))
    low_first, up_first = from_seq(first, 1), from_seq(first, -1)
    second = gate_rows(packed, packed, signal, query_rows, half, half)
    low_second, up_second = from_seq(second, 1), from_seq(second, -1)
    far = gate_rows(packed, far_before, far_signal, far_query, 0, 2 * half)
    done = whole_rows(first, second, far, full_weight)
    early_sum = half_rows(up_first, low_first, full_weight)
    return finish(z, done, early_sum, up_second, low_second, full_weight)


def solution(mesh):
    in_specs = (
        P(("seq", "chan"), None),
        P(("seq", "chan"), None),
        P(("seq", "chan"), None),
        P("chan", None),
        P("chan", None),
        P("chan"),
        P("chan", "seq"),
    )
    out_specs = P(None, "chan", "seq")
    return jax.shard_map(
        on_device, mesh=mesh, in_specs=in_specs, out_specs=out_specs, check_vma=False
    )
```

time: 895 us -> 118 us (0.13); the launches traced: 883 us -> 117 us
  other arithmetic: 333 us -> 0.72 us
  local copies, waits for them, and re-layouts: 292 us -> 7.38 us
  matrix products: 95.3 us -> 0 us
  waiting for transfers between devices: 103 us -> 8.45 us
  Pallas kernels: 0 us -> 26.9 us
  starting transfers between devices: 0.09 us -> 17.7 us
    slice x32 -> x1, local copies, waits for them, and re-layouts: 160 us -> 0.01 us  [on_device(): far_before = from_seq(packed[:, PARAMS:], 2)]
    sub x32 -> x0, other arithmetic: 149 us -> none  [the longest x16 149 us: packed_product(): real_out = left_real * right_real - inner_mask * left_imag * right_imag]
    while x64 -> x0, local copies, waits for them, and re-layouts: 110 us -> none
    add x17 -> x0, other arithmetic: 108 us -> none  [the longest x16 108 us: one_source(): return inner_sum + packed_product(window, source, block_len)]
    all_gather x3 -> x1, waiting for transfers between devices: 102 us -> 0.02 us  [on_device(): full_weight = lax.all_gather(out_weight, 'chan', axis=0, tiled=True)]
    dot_general x6 -> x0, matrix products: 95.3 us -> none  [the longest x1 31.7 us: lag_spectra(): jnp.einsum('kcm,rcm->krc', pole_terms, lag_weight, precision=precise)]
    mul x5 -> x0, other arithmetic: 34.8 us -> none  [the longest x1 34.7 us: inverse_matrix(): real_cols = scaling * jnp.cos(angles)]
    pallas_call x0 -> x9, Pallas kernels: none -> 26.9 us  [the longest x3 13.1 us: gate_rows(): call(gate_kernel, 'gate_rows', grid=(count,), in_specs=[pl.BlockSpec((ROW...]
  transfers between devices with their start and end apart: 3 -> 11, of which waited for: 2 -> 4; matrix products, arithmetic and copies ran while one was open for 9% -> 1% of each run, Pallas kernels for 0% -> 21%
where the time goes in v2:
time: 118 us; the launch traced here: 117 us
  blocking collectives  42.5 us (36%)
  Pallas kernels  26.9 us (23%)
  starting transfers between devices  17.7 us (15%)
  between operations  13.5 us (11%)
  waiting for transfers between devices  8.45 us (7%)
  local copies, waits for them, and re-layouts  7.38 us (6%)
    all_to_all x2, blocking collectives, to_owners(): lax.all_to_all(array, 'chan', split_axis=0, concat_axis=0, tiled=True)  42.5 us
    ppermute x10, starting transfers between devices, from_seq(): lax.ppermute(array, 'seq', [(i, (i + s) % seq_count) for i in range(seq_c...  17.7 us
    pallas_call x3, Pallas kernels, gate_rows(): call(gate_kernel, 'gate_rows', grid=(count,), in_specs=[pl.BlockSpec((ROW...  13.1 us
    ppermute x10, waiting for transfers between devices, from_seq(): lax.ppermute(array, 'seq', [(i, (i + s) % seq_count) for i in range(seq_c...  8.41 us
    unnamed x14, local copies, waits for them, and re-layouts  7.37 us
    pallas_call x1, Pallas kernels, make_signal(): call(signal_kernel, 'signal', limit=LARGE_LIMIT, grid=(width // GROUP,),...  3.63 us
    pallas_call x1, Pallas kernels, block_states(): call(functools.partial(states_kernel, tokens), 'block_states', grid=(bloc...  3.17 us
    pallas_call x1, Pallas kernels, half_rows(): call(half_kernel, 'half_rows', in_specs=[whole] * 3, out_specs=whole, out...  2.44 us
  transfers between devices with their start and end apart: 11, of which 4 were waited for; matrix products, arithmetic and copies ran while one was open for 1% of the time, Pallas kernels for 21%

profile of v2, /device:TPU:0, one launch (start us, length us, event | category | flops | bytes accessed | tf_op | source)
XLA Modules:
  0.0 117.2 jit_solution(9799252366221560798)
XLA Ops:
  6.5 4.0 %collective-permute-start = (bf16[128,4096]{1,0:T(8,128)(2,1)}, bf16[128,4096]{1,0:T(8,128)(2,1)S(1)}, u32[]{:S(2)}, u32[]{:S(2)}) collective-permute-start(bf16[128,4096]{1,0:T(8,128)(2,1)} %query_ref.3), channel_id=1, source_target_pairs={{0,64},{32,96},{64,0},{96,32},{1,65},{33,97},{65,1},{97,33},{2,66}... | collective-permute-start | bytes 3145736 | tf_op jit(solution)/shard_map/ppermute | solution.py:300
  10.5 3.6 %signal.1.signal_ref = bf16[32,128,128]{2,1,0:T(8,128)(2,1)} custom-call(bf16[128,4096]{1,0:T(8,128)(2,1)} %key_ref.1, bf16[128,4096]{1,0:T(8,128)(2,1)} %value_ref.1), custom_call_target="tpu_custom_call" | custom-call | flops 1024 | bytes 1024 | tf_op jit(solution)/shard_map/signal/pallas_call | solution.py:59
  14.1 24.1 %all_to_all.10.signal_ref = bf16[32,128,128]{2,1,0:T(8,128)(2,1)S(1)} all-to-all(bf16[32,128,128]{2,1,0:T(8,128)(2,1)} %signal.1.signal_ref), channel_id=1, replica_groups=mesh['seq'=4,'chan'=32] {'chan'}, dimensions={0} | all-to-all | bytes 2097152 | tf_op jit(solution)/shard_map/all_to_all | solution.py:303
  38.3 1.1 copy-done.4
  40.1 3.2 %block_states.1 = (f32[512,128]{1,0:T(8,128)S(1)}, f32[16,128]{1,0:T(8,128)S(1)}) custom-call(f32[16,128]{1,0:T(8,128)S(1)} %get-tuple-element.28.rate_ref, bf16[32,128,128]{2,1,0:T(8,128)(2,1)S(1)} %all_to_all.10.signal_ref), custom_call_target="tpu_custom_call" | custom-call | flops 1024 | bytes 1024 | tf_op jit(solution)/shard_map/block_states/pallas_call | solution.py:100
  43.3 1.1 collective-permute-start.1
  44.4 1.2 collective-permute-start.2
  45.5 1.6 %collective-permute-start.3 = (f32[16,128]{1,0:T(8,128)S(1)}, f32[16,128]{1,0:T(8,128)S(1)}, u32[]{:S(2)}, u32[]{:S(2)}) collective-permute-start(f32[16,128]{1,0:T(8,128)S(1)} %get-tuple-element.18), channel_id=1, source_target_pairs={{0,96},{32,0},{64,32},{96,64},{1,97},{33,1},{65,33},{97,65},{2,98}... | collective-permute-start | bytes 24584 | tf_op jit(solution)/shard_map/ppermute | solution.py:300
  47.1 1.1 collective-permute-done.1.refs_0_
  48.2 1.3 %collective-permute-done.2.refs_1_ = f32[16,128]{1,0:T(8,128)S(1)} collective-permute-done((f32[16,128]{1,0:T(8,128)S(1)}, f32[16,128]{1,0:T(8,128)S(1)}, u32[]{:S(2)}, u32[]{:S(2)}) %collective-permute-start.2) | collective-permute-done | bytes 8224 | tf_op jit(solution)/shard_map/ppermute | solution.py:300
  50.3 2.1 %collective-permute-start.4 = (bf16[32,128,128]{2,1,0:T(8,128)(2,1)}, bf16[32,128,128]{2,1,0:T(8,128)(2,1)S(1)}, u32[]{:S(2)}, u32[]{:S(2)}) collective-permute-start(bf16[32,128,128]{2,1,0:T(8,128)(2,1)} %signal.1.signal_ref), channel_id=1, source_target_pairs={{0,64},{32,96},{64,0},{96,32},{1,65},{33,97},{65,1},{97,33},{2,66}... | collective-permute-start | bytes 3145736 | tf_op jit(solution)/shard_map/ppermute | solution.py:300
  52.4 18.4 %all_to_all.11.packed_ref.before_ref = bf16[32,96,128]{2,1,0:T(8,128)(2,1)S(1)} all-to-all(bf16[32,96,128]{2,1,0:T(8,128)(2,1)S(1)} %states_before.1), channel_id=1, replica_groups=mesh['seq'=4,'chan'=32] {'chan'}, dimensions={0} | all-to-all | bytes 1572864 | tf_op jit(solution)/shard_map/all_to_all | solution.py:303
  70.7 5.3 %collective-permute-done.4.signal_ref = bf16[32,128,128]{2,1,0:T(8,128)(2,1)S(1)} collective-permute-done((bf16[32,128,128]{2,1,0:T(8,128)(2,1)}, bf16[32,128,128]{2,1,0:T(8,128)(2,1)S(1)}, u32[]{:S(2)}, u32[]{:S(2)}) %collective-permute-start.4) | collective-permute-done | bytes 1048608 | tf_op jit(solution)/shard_map/ppermute | solution.py:300
  76.1 2.1 %collective-permute-start.5 = (bf16[32,16,128]{2,1,0:T(8,128)(2,1)S(1)}, bf16[32,16,128]{2,1,0:T(8,128)(2,1)S(1)}, u32[]{:S(2)}, u32[]{:S(2)}) collective-permute-start(bf16[32,16,128]{2,1,0:T(8,128)(2,1)S(1)} %slice.3), channel_id=1, source_target_pairs={{0,64},{32,96},{64,0},{96,32},{1,65},{33,97},{65,1},{97,33},{2,66}... | collective-permute-start | bytes 393224 | tf_op jit(solution)/shard_map/ppermute | solution.py:300
  78.2 1.2 %copy-done.2 = bf16[32,128,128]{2,1,0:T(8,128)(2,1)S(1)} copy-done((bf16[32,128,128]{2,1,0:T(8,128)(2,1)S(1)}, bf16[32,128,128]{2,1,0:T(8,128)(2,1)}, u32[]{:S(2)}) %copy-start.2) | copy-done | bytes 1048600
  79.4 3.3 %gate_rows.3.first_ref = bf16[128,2048]{1,0:T(8,128)(2,1)S(1)} custom-call(bf16[32,96,128]{2,1,0:T(8,128)(2,1)S(1)} %all_to_all.11.packed_ref.before_ref, bf16[32,96,128]{2,1,0:T(8,128)(2,1)S(1)} %all_to_all.11.packed_ref.before_ref, bf16[32,128,128]{2,1,0:T(8,128)(2,1)S(1)} %copy-done.2, bf16[128,4096]{1,0:T(8,128)(2,1)S(1)} %copy-done.3), custom_call_target="tpu_custom_call" | custom-call | flops 1024 | bytes 1024 | tf_op jit(solution)/shard_map/gate_rows/pallas_call | solution.py:195
  82.7 2.4 %collective-permute-start.6 = (bf16[128,2048]{1,0:T(8,128)(2,1)S(1)}, bf16[128,2048]{1,0:T(8,128)(2,1)}, u32[]{:S(2)}, u32[]{:S(2)}) collective-permute-start(bf16[128,2048]{1,0:T(8,128)(2,1)S(1)} %gate_rows.3.first_ref), channel_id=1, source_target_pairs={{0,96},{32,0},{64,32},{96,64},{1,97},{33,1},{65,33},{97,65},{2,98}... | collective-permute-start | bytes 1572872 | tf_op jit(solution)/shard_map/ppermute | solution.py:300
  85.1 3.3 %gate_rows.4.second_ref = bf16[128,2048]{1,0:T(8,128)(2,1)S(1)} custom-call(bf16[32,96,128]{2,1,0:T(8,128)(2,1)S(1)} %all_to_all.11.packed_ref.before_ref, bf16[32,96,128]{2,1,0:T(8,128)(2,1)S(1)} %all_to_all.11.packed_ref.before_ref, bf16[32,128,128]{2,1,0:T(8,128)(2,1)S(1)} %copy-done.2, bf16[128,4096]{1,0:T(8,128)(2,1)S(1)} %copy-done.3), custom_call_target="tpu_custom_call" | custom-call | flops 1024 | bytes 1024 | tf_op jit(solution)/shard_map/gate_rows/pallas_call | solution.py:195
  88.4 3.3 %collective-permute-start.8 = (bf16[128,2048]{1,0:T(8,128)(2,1)S(1)}, bf16[128,2048]{1,0:T(8,128)(2,1)S(1)}, u32[]{:S(2)}, u32[]{:S(2)}) collective-permute-start(bf16[128,2048]{1,0:T(8,128)(2,1)S(1)} %gate_rows.4.second_ref), channel_id=1, source_target_pairs={{0,96},{32,0},{64,32},{96,64},{1,97},{33,1},{65,33},{97,65},{2,98}... | collective-permute-start | bytes 1572872 | tf_op jit(solution)/shard_map/ppermute | solution.py:300
  91.7 6.5 %gate_rows.5.far_ref = bf16[128,4096]{1,0:T(8,128)(2,1)S(1)} custom-call(bf16[32,96,128]{2,1,0:T(8,128)(2,1)S(1)} %all_to_all.11.packed_ref.before_ref, bf16[32,16,128]{2,1,0:T(8,128)(2,1)S(1)} %collective-permute-done.5.before_ref, bf16[32,128,128]{2,1,0:T(8,128)(2,1)S(1)} %collective-permute-done.4.signal_ref, bf16[128,4096]{1,0:T(8,128)(2,1)S(1)} %copy-done.5), custom_call_target="tpu_custom_call" | custom-call | flops 1024 | bytes 1024 | tf_op jit(solution)/shard_map/gate_rows/pallas_call | solution.py:195
  98.2 3.4 %copy-done = bf16[4096,1024]{1,0:T(8,128)(2,1)S(1)} copy-done((bf16[4096,1024]{1,0:T(8,128)(2,1)S(1)}, bf16[4096,1024]{1,0:T(8,128)(2,1)}, u32[]{:S(2)}) %copy-start) | copy-done | bytes 8388632
  101.6 2.3 %whole_rows.1.done_ref = bf16[256,1024]{1,0:T(8,128)(2,1)S(1)} custom-call(bf16[128,2048]{1,0:T(8,128)(2,1)S(1)} %gate_rows.3.first_ref, bf16[128,2048]{1,0:T(8,128)(2,1)S(1)} %gate_rows.4.second_ref, bf16[128,4096]{1,0:T(8,128)(2,1)S(1)} %gate_rows.5.far_ref, bf16[4096,1024]{1,0:T(8,128)(2,1)S(1)} %copy-done), custom_call_target="tpu_custom_call" | custom-call | flops 1024 | bytes 1024 | tf_op jit(solution)/shard_map/whole_rows/pallas_call | solution.py:229
  105.0 2.4 %half_rows.1.sum_ref = f32[256,1024]{1,0:T(8,128)S(1)} custom-call(bf16[128,2048]{1,0:T(8,128)(2,1)} %collective-permute-done.6.upper_ref, bf16[128,2048]{1,0:T(8,128)(2,1)} %collective-permute-done.7.lower_ref, bf16[4096,1024]{1,0:T(8,128)(2,1)S(1)} %copy-done.1), custom_call_target="tpu_custom_call" | custom-call | flops 1024 | bytes 1024 | tf_op jit(solution)/shard_map/half_rows/pallas_call | solution.py:253
  108.1 2.2 %finish.1 = bf16[4,128,1024]{2,1,0:T(8,128)(2,1)} custom-call(s32[1]{0:T(128)} %bitcast.place_ref, bf16[256,1024]{1,0:T(8,128)(2,1)S(1)} %whole_rows.1.done_ref, f32[256,1024]{1,0:T(8,128)S(1)} %half_rows.1.sum_ref, bf16[128,2048]{1,0:T(8,128)(2,1)S(1)} %collective-permute-done.8.upper_ref, bf16[128,2048]{1,0:T(8,128)(2,1)S(1)} %collective-permute-done.9.lower_ref, ...), custom_call_target="tpu_custom_call" | custom-call | flops 1024 | bytes 1024 | tf_op jit(solution)/shard_map/finish/pallas_call | solution.py:282
  (26 shorter events, 3.3 us)
Async XLA Ops:
  6.5 71.6 %copy-start.3 = (bf16[128,4096]{1,0:T(8,128)(2,1)S(1)}, bf16[128,4096]{1,0:T(8,128)(2,1)}, u32[]{:S(2)}) copy-start(bf16[128,4096]{1,0:T(8,128)(2,1)} %query_ref.3) | copy-start | bytes 3145732
  6.5 91.7 %all-gather.2.cloned.1.call-start = ((), (), s32[]{:S(2)}) async-start(), calls=%async_computation.2 | async-start | bytes 8650752 | tf_op jit(solution)/shard_map/all_gather | solution.py:312
  6.5 31.7 %collective-permute-start = (bf16[128,4096]{1,0:T(8,128)(2,1)}, bf16[128,4096]{1,0:T(8,128)(2,1)S(1)}, u32[]{:S(2)}, u32[]{:S(2)}) collective-permute-start(bf16[128,4096]{1,0:T(8,128)(2,1)} %query_ref.3), channel_id=1, source_target_pairs={{0,64},{32,96},{64,0},{96,32},{1,65},{33,97},{65,1},{97,33},{2,66}... | collective-permute-start | bytes 3145736 | tf_op jit(solution)/shard_map/ppermute | solution.py:300
  38.3 1.1 copy-start.4
  43.3 4.9 %collective-permute-start.1 = (f32[16,128]{1,0:T(8,128)S(1)}, f32[16,128]{1,0:T(8,128)S(1)}, u32[]{:S(2)}, u32[]{:S(2)}) collective-permute-start(f32[16,128]{1,0:T(8,128)S(1)} %get-tuple-element.18), channel_id=1, source_target_pairs={{0,32},{32,64},{64,96},{96,0},{1,33},{33,65},{65,97},{97,1},{2,34}... | collective-permute-start | bytes 24584 | tf_op jit(solution)/shard_map/ppermute | solution.py:300
  44.4 5.2 %collective-permute-start.2 = (f32[16,128]{1,0:T(8,128)S(1)}, f32[16,128]{1,0:T(8,128)S(1)}, u32[]{:S(2)}, u32[]{:S(2)}) collective-permute-start(f32[16,128]{1,0:T(8,128)S(1)} %get-tuple-element.18), channel_id=1, source_target_pairs={{0,64},{32,96},{64,0},{96,32},{1,65},{33,97},{65,1},{97,33},{2,66}... | collective-permute-start | bytes 24584 | tf_op jit(solution)/shard_map/ppermute | solution.py:300
  45.5 4.0 %collective-permute-start.3 = (f32[16,128]{1,0:T(8,128)S(1)}, f32[16,128]{1,0:T(8,128)S(1)}, u32[]{:S(2)}, u32[]{:S(2)}) collective-permute-start(f32[16,128]{1,0:T(8,128)S(1)} %get-tuple-element.18), channel_id=1, source_target_pairs={{0,96},{32,0},{64,32},{96,64},{1,97},{33,1},{65,33},{97,65},{2,98}... | collective-permute-start | bytes 24584 | tf_op jit(solution)/shard_map/ppermute | solution.py:300
  47.1 44.5 %copy-start.5 = (bf16[128,4096]{1,0:T(8,128)(2,1)S(1)}, bf16[128,4096]{1,0:T(8,128)(2,1)}, u32[]{:S(2)}) copy-start(bf16[128,4096]{1,0:T(8,128)(2,1)} %copy-done.4) | copy-start | bytes 3145732
  49.5 0.7 copy-start.6
  50.3 25.8 %collective-permute-start.4 = (bf16[32,128,128]{2,1,0:T(8,128)(2,1)}, bf16[32,128,128]{2,1,0:T(8,128)(2,1)S(1)}, u32[]{:S(2)}, u32[]{:S(2)}) collective-permute-start(bf16[32,128,128]{2,1,0:T(8,128)(2,1)} %signal.1.signal_ref), channel_id=1, source_target_pairs={{0,64},{32,96},{64,0},{96,32},{1,65},{33,97},{65,1},{97,33},{2,66}... | collective-permute-start | bytes 3145736 | tf_op jit(solution)/shard_map/ppermute | solution.py:300
  76.1 6.6 %collective-permute-start.5 = (bf16[32,16,128]{2,1,0:T(8,128)(2,1)S(1)}, bf16[32,16,128]{2,1,0:T(8,128)(2,1)S(1)}, u32[]{:S(2)}, u32[]{:S(2)}) collective-permute-start(bf16[32,16,128]{2,1,0:T(8,128)(2,1)S(1)} %slice.3), channel_id=1, source_target_pairs={{0,64},{32,96},{64,0},{96,32},{1,65},{33,97},{65,1},{97,33},{2,66}... | collective-permute-start | bytes 393224 | tf_op jit(solution)/shard_map/ppermute | solution.py:300
  78.2 1.2 %copy-start.2 = (bf16[32,128,128]{2,1,0:T(8,128)(2,1)S(1)}, bf16[32,128,128]{2,1,0:T(8,128)(2,1)}, u32[]{:S(2)}) copy-start(bf16[32,128,128]{2,1,0:T(8,128)(2,1)} %signal.1.signal_ref) | copy-start | bytes 3145732
  82.7 21.2 %collective-permute-start.6 = (bf16[128,2048]{1,0:T(8,128)(2,1)S(1)}, bf16[128,2048]{1,0:T(8,128)(2,1)}, u32[]{:S(2)}, u32[]{:S(2)}) collective-permute-start(bf16[128,2048]{1,0:T(8,128)(2,1)S(1)} %gate_rows.3.first_ref), channel_id=1, source_target_pairs={{0,96},{32,0},{64,32},{96,64},{1,97},{33,1},{65,33},{97,65},{2,98}... | collective-permute-start | bytes 1572872 | tf_op jit(solution)/shard_map/ppermute | solution.py:300
  85.1 18.9 %collective-permute-start.7 = (bf16[128,2048]{1,0:T(8,128)(2,1)S(1)}, bf16[128,2048]{1,0:T(8,128)(2,1)}, u32[]{:S(2)}, u32[]{:S(2)}) collective-permute-start(bf16[128,2048]{1,0:T(8,128)(2,1)S(1)} %gate_rows.3.first_ref), channel_id=1, source_target_pairs={{0,32},{32,64},{64,96},{96,0},{1,33},{33,65},{65,97},{97,1},{2,34}... | collective-permute-start | bytes 1572872 | tf_op jit(solution)/shard_map/ppermute | solution.py:300
  88.4 19.1 %collective-permute-start.8 = (bf16[128,2048]{1,0:T(8,128)(2,1)S(1)}, bf16[128,2048]{1,0:T(8,128)(2,1)S(1)}, u32[]{:S(2)}, u32[]{:S(2)}) collective-permute-start(bf16[128,2048]{1,0:T(8,128)(2,1)S(1)} %gate_rows.4.second_ref), channel_id=1, source_target_pairs={{0,96},{32,0},{64,32},{96,64},{1,97},{33,1},{65,33},{97,65},{2,98}... | collective-permute-start | bytes 1572872 | tf_op jit(solution)/shard_map/ppermute | solution.py:300
  91.7 16.5 %collective-permute-start.9 = (bf16[128,2048]{1,0:T(8,128)(2,1)S(1)}, bf16[128,2048]{1,0:T(8,128)(2,1)S(1)}, u32[]{:S(2)}, u32[]{:S(2)}) collective-permute-start(bf16[128,2048]{1,0:T(8,128)(2,1)S(1)} %gate_rows.4.second_ref), channel_id=1, source_target_pairs={{0,32},{32,64},{64,96},{96,0},{1,33},{33,65},{65,97},{97,1},{2,34}... | collective-permute-start | bytes 1572872 | tf_op jit(solution)/shard_map/ppermute | solution.py:300
  98.2 3.4 %copy-start = (bf16[4096,1024]{1,0:T(8,128)(2,1)S(1)}, bf16[4096,1024]{1,0:T(8,128)(2,1)}, u32[]{:S(2)}) copy-start(bf16[4096,1024]{1,0:T(8,128)(2,1)} %all-gather.2.cloned.1.call-done.matrix_ref) | copy-start | bytes 25165828
  101.6 3.4 %copy-start.1 = (bf16[4096,1024]{1,0:T(8,128)(2,1)S(1)}, bf16[4096,1024]{1,0:T(8,128)(2,1)}, u32[]{:S(2)}) copy-start(bf16[4096,1024]{1,0:T(8,128)(2,1)} %all-gather.2.cloned.1.call-done.matrix_ref) | copy-start | bytes 25165828
Sparse Core Ops, SparseCore 0:
  39.5 56.0 all-gather.1

commit v3 on v2

--- a/solution.py
+++ b/solution.py
@@ -12,18 +12,19 @@
 ROWS = 8
 GROUP = ROWS * LANES
 UNROLL = 8
+SLICE = 32
 PARAMS = 5 * ORDER
 SMALL_LIMIT = 16 * 1024 * 1024
 LARGE_LIMIT = 56 * 1024 * 1024
 COLUMNS = 256
 
 
-def call(kernel, name, limit=SMALL_LIMIT, **keywords):
+def call(kernel, name, limit=SMALL_LIMIT, moved=1024, **keywords):
     return pl.pallas_call(
         kernel,
         name=name,
         compiler_params=pltpu.CompilerParams(vmem_limit_bytes=limit),
-        cost_estimate=pl.CostEstimate(flops=1024, bytes_accessed=1024, transcendentals=0),
+        cost_estimate=pl.CostEstimate(flops=1024, bytes_accessed=moved, transcendentals=0),
         **keywords,
     )
 
@@ -47,23 +48,39 @@
     return lax.fori_loop(0, tokens // UNROLL, several, held)
 
 
-def signal_kernel(key_ref, value_ref, signal_ref):
-    signal = (as_float(key_ref[...]) * as_float(value_ref[...])).astype(jnp.bfloat16)
-    for j in range(ROWS):
-        signal_ref[j] = signal[:, j * LANES : (j + 1) * LANES]
+def signal_kernel(key_hbm, value_hbm, signal_ref, key_ref, value_ref, sems):
+    parts = sems.shape[1]
+    size = key_ref.shape[0] // parts
+    copies = []
+    for n in range(parts):
+        rows = pl.ds(n * size, size)
+        for at, (source, target) in enumerate([(key_hbm, key_ref), (value_hbm, value_ref)]):
+            copies.append(pltpu.make_async_copy(source.at[rows, :], target.at[rows, :], sems.at[at, n]))
+            copies[-1].start()
+    for n in range(parts):
+        copies[2 * n].wait()
+        copies[2 * n + 1].wait()
+        rows = slice(n * size, (n + 1) * size)
+        for j in range(signal_ref.shape[0]):
+            columns = slice(j * LANES, (j + 1) * LANES)
+            product = as_float(key_ref[rows, columns]) * as_float(value_ref[rows, columns])
+            signal_ref[j, rows, :] = product.astype(jnp.bfloat16)
 
 
 def make_signal(key_rows, value_rows):
     tokens, width = key_rows.shape
-    natural = pl.BlockSpec((tokens, GROUP), lambda g: (0, g))
+    outside = pl.BlockSpec(memory_space=pltpu.HBM)
     return call(
         signal_kernel,
         "signal",
-        limit=LARGE_LIMIT,
-        grid=(width // GROUP,),
-        in_specs=[natural, natural],
-        out_specs=pl.BlockSpec((ROWS, tokens, LANES), lambda g: (g, 0, 0)),
+        in_specs=[outside, outside],
+        out_specs=pl.BlockSpec(memory_space=pltpu.VMEM),
         out_shape=jax.ShapeDtypeStruct((width // LANES, tokens, LANES), jnp.bfloat16),
+        scratch_shapes=[
+            pltpu.VMEM((tokens, width), jnp.bfloat16),
+            pltpu.VMEM((tokens, width), jnp.bfloat16),
+            pltpu.SemaphoreType.DMA((2, tokens // SLICE)),
+        ],
     )(key_rows, value_rows)
 
 
@@ -189,12 +206,13 @@
         gated_ref[:, columns] = gated.astype(jnp.bfloat16)
 
 
-def gate_rows(packed, before, signal, query, first, count):
+def gate_rows(packed, before, signal, query, first, count, moved=1024):
     tokens = query.shape[0]
     last = before.shape[1] // ORDER - 1
     return call(
         gate_kernel,
         "gate_rows",
+        moved=moved,
         grid=(count,),
         in_specs=[
             pl.BlockSpec((ROWS, PARAMS, LANES), lambda g: (g + first, 0, 0)),
@@ -212,52 +230,39 @@
     )(packed, before, signal, query)
 
 
-def whole_kernel(first_ref, second_ref, far_ref, matrix_ref, out_ref, rows_ref):
+def early_kernel(first_ref, second_ref, far_ref, upper_ref, lower_ref, matrix_ref, done_ref, sum_ref, rows_ref, half_ref):
     tokens, split = first_ref.shape
     rows_ref[:tokens, :split] = first_ref[...]
     rows_ref[:tokens, split:] = second_ref[...]
     rows_ref[tokens:, :] = far_ref[...]
-    for n in range(0, out_ref.shape[1], COLUMNS):
+    half_ref[:tokens, :] = upper_ref[...]
+    half_ref[tokens:, :] = lower_ref[...]
+    for n in range(0, done_ref.shape[1], COLUMNS):
         columns = slice(n, n + COLUMNS)
         product = jnp.dot(rows_ref[...], matrix_ref[:, columns], preferred_element_type=jnp.float32)
-        out_ref[:, columns] = product.astype(jnp.bfloat16)
-
-
-def whole_rows(first, second, far, matrix):
+        done_ref[:, columns] = product.astype(jnp.bfloat16)
+        sum_ref[:, columns] = jnp.dot(
+            half_ref[...], matrix_ref[:split, columns], preferred_element_type=jnp.float32
+        )
+
+
+def early_rows(first, second, far, upper, lower, matrix):
     whole = pl.BlockSpec(memory_space=pltpu.VMEM)
     tokens, columns = far.shape[0], matrix.shape[1]
     return call(
-        whole_kernel,
-        "whole_rows",
-        in_specs=[whole] * 4,
-        out_specs=whole,
-        out_shape=jax.ShapeDtypeStruct((2 * tokens, columns), jnp.bfloat16),
-        scratch_shapes=[pltpu.VMEM((2 * tokens, far.shape[1]), jnp.bfloat16)],
-    )(first, second, far, matrix)
-
-
-def half_kernel(upper_ref, lower_ref, matrix_ref, sum_ref, rows_ref):
-    tokens, depth = upper_ref.shape
-    rows_ref[:tokens, :] = upper_ref[...]
-    rows_ref[tokens:, :] = lower_ref[...]
-    for n in range(0, sum_ref.shape[1], COLUMNS):
-        columns = slice(n, n + COLUMNS)
-        sum_ref[:, columns] = jnp.dot(
-            rows_ref[...], matrix_ref[:depth, columns], preferred_element_type=jnp.float32
-        )
-
-
-def half_rows(upper, lower, matrix):
-    whole = pl.BlockSpec(memory_space=pltpu.VMEM)
-    tokens, depth = upper.shape
-    return call(
-        half_kernel,
-        "half_rows",
-        in_specs=[whole] * 3,
-        out_specs=whole,
-        out_shape=jax.ShapeDtypeStruct((2 * tokens, matrix.shape[1]), jnp.float32),
-        scratch_shapes=[pltpu.VMEM((2 * tokens, depth), jnp.bfloat16)],
-    )(upper, lower, matrix)
+        early_kernel,
+        "early_rows",
+        in_specs=[whole] * 6,
+        out_specs=[whole] * 2,
+        out_shape=[
+            jax.ShapeDtypeStruct((2 * tokens, columns), jnp.bfloat16),
+            jax.ShapeDtypeStruct((2 * tokens, columns), jnp.float32),
+        ],
+        scratch_shapes=[
+            pltpu.VMEM((2 * tokens, far.shape[1]), jnp.bfloat16),
+            pltpu.VMEM((2 * tokens, first.shape[1]), jnp.bfloat16),
+        ],
+    )(first, second, far, upper, lower, matrix)
 
 
 def finish_kernel(place_ref, done_ref, sum_ref, upper_ref, lower_ref, matrix_ref, out_ref, rows_ref):
@@ -313,21 +318,19 @@
 
     prefix, total = block_states(tokens, rate, received)
     totals = [from_seq(total, s) for s in (1, 2, 3)]
+    totals, signal = lax.optimization_barrier((totals, signal))
+    far_signal = from_seq(signal, 2)
     packed = states_before(tokens, z, rate, weight, skip_gain[None, :], prefix, totals)
-    packed, signal = lax.optimization_barrier((packed, signal))
-    far_signal = from_seq(signal, 2)
     packed = to_owners(packed)
-    packed, far_signal = lax.optimization_barrier((packed, far_signal))
-
     far_before = from_seq(packed[:, PARAMS:], 2)
     first = gate_rows(packed, packed, signal, query_rows, 0, half)
-    first, far_before = lax.optimization_barrier((first, far_before))
+    first, far_before, far_signal = lax.optimization_barrier((first, far_before, far_signal))
     low_first, up_first = from_seq(first, 1), from_seq(first, -1)
     second = gate_rows(packed, packed, signal, query_rows, half, half)
     low_second, up_second = from_seq(second, 1), from_seq(second, -1)
-    far = gate_rows(packed, far_before, far_signal, far_query, 0, 2 * half)
-    done = whole_rows(first, second, far, full_weight)
-    early_sum = half_rows(up_first, low_first, full_weight)
+    second, far_before = lax.optimization_barrier((second, far_before))
+    far = gate_rows(packed, far_before, far_signal, far_query, 0, 2 * half, 20 * 1024 * 1024)
+    done, early_sum = early_rows(first, second, far, up_first, low_first, full_weight)
     return finish(z, done, early_sum, up_second, low_second, full_weight)
 
 

time: 118 us -> 116 us (0.983)
  local copies, waits for them, and re-layouts: 7.38 us -> 11.3 us
  Pallas kernels: 26.9 us -> 23.3 us
  waiting for transfers between devices: 8.45 us -> 5.95 us
  starting transfers between devices: 17.7 us -> 16.3 us
    unnamed x14 -> x24, local copies, waits for them, and re-layouts: 7.37 us -> 11.3 us
    pallas_call x6 -> x5, Pallas kernels: 21.4 us -> 17.8 us  [the longest x3 13.9 us: gate_rows(): call(gate_kernel, 'gate_rows', moved=moved, grid=(count,), in_specs=[pl.B...]
    ppermute x10, waiting for transfers between devices: 8.41 us -> 5.93 us  [from_seq(): lax.ppermute(array, 'seq', [(i, (i + s) % seq_count) for i in range(seq_c...]
    ppermute x10, starting transfers between devices: 17.7 us -> 16.3 us  [from_seq(): lax.ppermute(array, 'seq', [(i, (i + s) % seq_count) for i in range(seq_c...]
  transfers between devices with their start and end apart: 11 -> 11, of which waited for: 4 -> 4; matrix products, arithmetic and copies ran while one was open for 1% -> 1% of each run, Pallas kernels for 21% -> 18%
where the time goes in v3:
time: 116 us; the launch traced here: 114 us
  blocking collectives  43.2 us (37%)
  Pallas kernels  23.3 us (20%)
  starting transfers between devices  16.3 us (14%)
  between operations  13.5 us (12%)
  local copies, waits for them, and re-layouts  11.3 us (10%)
  waiting for transfers between devices  5.95 us (5%)
    all_to_all x2, blocking collectives, to_owners(): lax.all_to_all(array, 'chan', split_axis=0, concat_axis=0, tiled=True)  43.2 us
    ppermute x10, starting transfers between devices, from_seq(): lax.ppermute(array, 'seq', [(i, (i + s) % seq_count) for i in range(seq_c...  16.3 us
    pallas_call x3, Pallas kernels, gate_rows(): call(gate_kernel, 'gate_rows', moved=moved, grid=(count,), in_specs=[pl.B...  13.9 us
    unnamed x24, local copies, waits for them, and re-layouts  11.3 us
    ppermute x10, waiting for transfers between devices, from_seq(): lax.ppermute(array, 'seq', [(i, (i + s) % seq_count) for i in range(seq_c...  5.93 us
    pallas_call x1, Pallas kernels, early_rows(): call(early_kernel, 'early_rows', in_specs=[whole] * 6, out_specs=[whole]...  3.42 us
    pallas_call x1, Pallas kernels, block_states(): call(functools.partial(states_kernel, tokens), 'block_states', grid=(bloc...  3.17 us
  transfers between devices with their start and end apart: 11, of which 4 were waited for; matrix products, arithmetic and copies ran while one was open for 1% of the time, Pallas kernels for 18%

profile of v3, /device:TPU:0, one launch (start us, length us, event | category | flops | bytes accessed | tf_op | source)
XLA Modules:
  0.0 114.3 jit_solution(15182362569784685531)
XLA Ops:
  6.5 4.0 %collective-permute-start = (bf16[128,4096]{1,0:T(8,128)(2,1)}, bf16[128,4096]{1,0:T(8,128)(2,1)S(1)}, u32[]{:S(2)}, u32[]{:S(2)}) collective-permute-start(bf16[128,4096]{1,0:T(8,128)(2,1)} %query_ref.3), channel_id=1, source_target_pairs={{0,64},{32,96},{64,0},{96,32},{1,65},{33,97},{65,1},{97,33},{2,66}... | collective-permute-start | bytes 3145736 | tf_op jit(solution)/shard_map/ppermute | solution.py:305
  10.5 1.2 %copy-done.3 = bf16[128,4096]{1,0:T(8,128)(2,1)S(1)} copy-done((bf16[128,4096]{1,0:T(8,128)(2,1)S(1)}, bf16[128,4096]{1,0:T(8,128)(2,1)}, u32[]{:S(2)}) %copy-start.3) | copy-done | bytes 1048600
  11.7 1.2 %copy-done.4 = bf16[128,4096]{1,0:T(8,128)(2,1)S(1)} copy-done((bf16[128,4096]{1,0:T(8,128)(2,1)S(1)}, bf16[128,4096]{1,0:T(8,128)(2,1)}, u32[]{:S(2)}) %copy-start.4) | copy-done | bytes 1048600
  13.4 23.9 %all_to_all.10.signal_ref = bf16[32,128,128]{2,1,0:T(8,128)(2,1)S(1)} all-to-all(bf16[32,128,128]{2,1,0:T(8,128)(2,1)S(1)} %signal.1.signal_ref), channel_id=1, replica_groups=mesh['seq'=4,'chan'=32] {'chan'}, dimensions={0} | all-to-all | bytes 2097152 | tf_op jit(solution)/shard_map/all_to_all | solution.py:308
  39.1 3.2 %block_states.1 = (f32[512,128]{1,0:T(8,128)S(1)}, f32[16,128]{1,0:T(8,128)S(1)}) custom-call(f32[16,128]{1,0:T(8,128)S(1)} %get-tuple-element.38.rate_ref, bf16[32,128,128]{2,1,0:T(8,128)(2,1)S(1)} %all_to_all.10.signal_ref), custom_call_target="tpu_custom_call" | custom-call | flops 1024 | bytes 1024 | tf_op jit(solution)/shard_map/block_states/pallas_call | solution.py:117
  42.3 1.1 collective-permute-start.1
  43.4 1.2 %collective-permute-start.2 = (f32[16,128]{1,0:T(8,128)S(1)}, f32[16,128]{1,0:T(8,128)S(1)}, u32[]{:S(2)}, u32[]{:S(2)}) collective-permute-start(f32[16,128]{1,0:T(8,128)S(1)} %get-tuple-element.23), channel_id=1, source_target_pairs={{0,64},{32,96},{64,0},{96,32},{1,65},{33,97},{65,1},{97,33},{2,66}... | collective-permute-start | bytes 24584 | tf_op jit(solution)/shard_map/ppermute | solution.py:305
  44.5 1.6 %collective-permute-start.3 = (f32[16,128]{1,0:T(8,128)S(1)}, f32[16,128]{1,0:T(8,128)S(1)}, u32[]{:S(2)}, u32[]{:S(2)}) collective-permute-start(f32[16,128]{1,0:T(8,128)S(1)} %get-tuple-element.23), channel_id=1, source_target_pairs={{0,96},{32,0},{64,32},{96,64},{1,97},{33,1},{65,33},{97,65},{2,98}... | collective-permute-start | bytes 24584 | tf_op jit(solution)/shard_map/ppermute | solution.py:305
  46.1 1.1 collective-permute-done.1.refs_0_
  47.2 1.3 %collective-permute-done.2.refs_1_ = f32[16,128]{1,0:T(8,128)S(1)} collective-permute-done((f32[16,128]{1,0:T(8,128)S(1)}, f32[16,128]{1,0:T(8,128)S(1)}, u32[]{:S(2)}, u32[]{:S(2)}) %collective-permute-start.2) | collective-permute-done | bytes 8224 | tf_op jit(solution)/shard_map/ppermute | solution.py:305
  48.5 2.0 %collective-permute-start.5 = (bf16[32,128,128]{2,1,0:T(8,128)(2,1)S(1)}, bf16[32,128,128]{2,1,0:T(8,128)(2,1)}, u32[]{:S(2)}, u32[]{:S(2)}) collective-permute-start(bf16[32,128,128]{2,1,0:T(8,128)(2,1)S(1)} %signal.1.signal_ref), channel_id=1, source_target_pairs={{0,64},{32,96},{64,0},{96,32},{1,65},{33,97},{65,1},{97,33},{2,66}... | collective-permute-start | bytes 3145736 | tf_op jit(solution)/shard_map/ppermute | solution.py:305
  51.4 19.3 %all_to_all.11.packed_ref.before_ref = bf16[32,96,128]{2,1,0:T(8,128)(2,1)S(1)} all-to-all(bf16[32,96,128]{2,1,0:T(8,128)(2,1)S(1)} %states_before.1), channel_id=1, replica_groups=mesh['seq'=4,'chan'=32] {'chan'}, dimensions={0} | all-to-all | bytes 1572864 | tf_op jit(solution)/shard_map/all_to_all | solution.py:308
  70.7 2.1 %collective-permute-start.4 = (bf16[32,16,128]{2,1,0:T(8,128)(2,1)S(1)}, bf16[32,16,128]{2,1,0:T(8,128)(2,1)S(1)}, u32[]{:S(2)}, u32[]{:S(2)}) collective-permute-start(bf16[32,16,128]{2,1,0:T(8,128)(2,1)S(1)} %slice.4), channel_id=1, source_target_pairs={{0,64},{32,96},{64,0},{96,32},{1,65},{33,97},{65,1},{97,33},{2,66}... | collective-permute-start | bytes 393224 | tf_op jit(solution)/shard_map/ppermute | solution.py:305
  72.8 3.3 %gate_rows.3.first_ref = bf16[128,2048]{1,0:T(8,128)(2,1)S(1)} custom-call(bf16[32,96,128]{2,1,0:T(8,128)(2,1)S(1)} %all_to_all.11.packed_ref.before_ref, bf16[32,96,128]{2,1,0:T(8,128)(2,1)S(1)} %all_to_all.11.packed_ref.before_ref, bf16[32,128,128]{2,1,0:T(8,128)(2,1)S(1)} %signal.1.signal_ref, bf16[128,4096]{1,0:T(8,128)(2,1)S(1)} %copy-done.2), custom_call_target="tpu_custom_call" | custom-call | flops 1024 | bytes 1024 | tf_op jit(solution)/shard_map/gate_rows/pallas_call | solution.py:212
  76.0 2.3 %collective-permute-done.4.before_ref = bf16[32,16,128]{2,1,0:T(8,128)(2,1)S(1)} collective-permute-done((bf16[32,16,128]{2,1,0:T(8,128)(2,1)S(1)}, bf16[32,16,128]{2,1,0:T(8,128)(2,1)S(1)}, u32[]{:S(2)}, u32[]{:S(2)}) %collective-permute-start.4) | collective-permute-done | bytes 131104 | tf_op jit(solution)/shard_map/ppermute | solution.py:305
  80.3 3.3 %gate_rows.4.second_ref = bf16[128,2048]{1,0:T(8,128)(2,1)S(1)} custom-call(bf16[32,96,128]{2,1,0:T(8,128)(2,1)S(1)} %all_to_all.11.packed_ref.before_ref, bf16[32,96,128]{2,1,0:T(8,128)(2,1)S(1)} %all_to_all.11.packed_ref.before_ref, bf16[32,128,128]{2,1,0:T(8,128)(2,1)S(1)} %signal.1.signal_ref, bf16[128,4096]{1,0:T(8,128)(2,1)S(1)} %copy-done.2), custom_call_target="tpu_custom_call" | custom-call | flops 1024 | bytes 1024 | tf_op jit(solution)/shard_map/gate_rows/pallas_call | solution.py:212
  83.6 2.3 %collective-permute-start.8 = (bf16[128,2048]{1,0:T(8,128)(2,1)S(1)}, bf16[128,2048]{1,0:T(8,128)(2,1)S(1)}, u32[]{:S(2)}, u32[]{:S(2)}) collective-permute-start(bf16[128,2048]{1,0:T(8,128)(2,1)S(1)} %gate_rows.4.second_ref), channel_id=1, source_target_pairs={{0,96},{32,0},{64,32},{96,64},{1,97},{33,1},{65,33},{97,65},{2,98}... | collective-permute-start | bytes 1572872 | tf_op jit(solution)/shard_map/ppermute | solution.py:305
  85.9 7.4 %gate_rows.5.far_ref = bf16[128,4096]{1,0:T(8,128)(2,1)S(1)} custom-call(bf16[32,96,128]{2,1,0:T(8,128)(2,1)S(1)} %all_to_all.11.packed_ref.before_ref, bf16[32,16,128]{2,1,0:T(8,128)(2,1)S(1)} %collective-permute-done.4.before_ref, bf16[32,128,128]{2,1,0:T(8,128)(2,1)} %collective-permute-done.5.signal_ref, bf16[128,4096]{1,0:T(8,128)(2,1)S(1)} %copy-done.6), custom_call_target="tpu_custom_call" | custom-call | flops 1024 | bytes 20971520 | tf_op jit(solution)/shard_map/gate_rows/pallas_call | solution.py:212
  94.1 1.3 %collective-permute-done.7.lower_ref = bf16[128,2048]{1,0:T(8,128)(2,1)S(1)} collective-permute-done((bf16[128,2048]{1,0:T(8,128)(2,1)S(1)}, bf16[128,2048]{1,0:T(8,128)(2,1)S(1)}, u32[]{:S(2)}, u32[]{:S(2)}) %collective-permute-start.7) | collective-permute-done | bytes 524320 | tf_op jit(solution)/shard_map/ppermute | solution.py:305
  96.3 3.4 %copy-done = bf16[4096,1024]{1,0:T(8,128)(2,1)S(1)} copy-done((bf16[4096,1024]{1,0:T(8,128)(2,1)S(1)}, bf16[4096,1024]{1,0:T(8,128)(2,1)}, u32[]{:S(2)}) %copy-start) | copy-done | bytes 8388632
  99.7 1.0 copy-done.8
  100.7 1.0 copy-done.10
  101.7 3.4 %early_rows.1 = (bf16[256,1024]{1,0:T(8,128)(2,1)S(1)}, f32[256,1024]{1,0:T(8,128)S(1)}) custom-call(bf16[128,2048]{1,0:T(8,128)(2,1)S(1)} %gate_rows.3.first_ref, bf16[128,2048]{1,0:T(8,128)(2,1)S(1)} %gate_rows.4.second_ref, bf16[128,4096]{1,0:T(8,128)(2,1)S(1)} %gate_rows.5.far_ref, bf16[128,2048]{1,0:T(8,128)(2,1)S(1)} %copy-done.8, ...), custom_call_target="tpu_custom_call" | custom-call | flops 1024 | bytes 1024 | tf_op jit(solution)/shard_map/early_rows/pallas_call | solution.py:252
  105.2 2.2 %finish.1 = bf16[4,128,1024]{2,1,0:T(8,128)(2,1)} custom-call(s32[1]{0:T(128)} %bitcast.place_ref, bf16[256,1024]{1,0:T(8,128)(2,1)S(1)} %get-tuple-element.35.done_ref, f32[256,1024]{1,0:T(8,128)S(1)} %get-tuple-element.36.sum_ref, bf16[128,2048]{1,0:T(8,128)(2,1)S(1)} %collective-permute-done.8.upper_ref, ...), custom_call_target="tpu_custom_call" | custom-call | flops 1024 | bytes 1024 | tf_op jit(solution)/shard_map/finish/pallas_call | solution.py:287
  (35 shorter events, 6.7 us)
Async XLA Ops:
  6.5 66.2 %copy-start.2 = (bf16[128,4096]{1,0:T(8,128)(2,1)S(1)}, bf16[128,4096]{1,0:T(8,128)(2,1)}, u32[]{:S(2)}) copy-start(bf16[128,4096]{1,0:T(8,128)(2,1)} %query_ref.3) | copy-start | bytes 3145732
  6.5 89.7 %all-gather.2.cloned.1.call-start = ((), (), s32[]{:S(2)}) async-start(), calls=%async_computation.2 | async-start | bytes 8650752 | tf_op jit(solution)/shard_map/all_gather | solution.py:317
  6.5 30.8 %collective-permute-start = (bf16[128,4096]{1,0:T(8,128)(2,1)}, bf16[128,4096]{1,0:T(8,128)(2,1)S(1)}, u32[]{:S(2)}, u32[]{:S(2)}) collective-permute-start(bf16[128,4096]{1,0:T(8,128)(2,1)} %query_ref.3), channel_id=1, source_target_pairs={{0,64},{32,96},{64,0},{96,32},{1,65},{33,97},{65,1},{97,33},{2,66}... | collective-permute-start | bytes 3145736 | tf_op jit(solution)/shard_map/ppermute | solution.py:305
  10.5 1.2 %copy-start.3 = (bf16[128,4096]{1,0:T(8,128)(2,1)S(1)}, bf16[128,4096]{1,0:T(8,128)(2,1)}, u32[]{:S(2)}) copy-start(bf16[128,4096]{1,0:T(8,128)(2,1)} %key_hbm.1) | copy-start | bytes 3145732
  11.7 1.2 %copy-start.4 = (bf16[128,4096]{1,0:T(8,128)(2,1)S(1)}, bf16[128,4096]{1,0:T(8,128)(2,1)}, u32[]{:S(2)}) copy-start(bf16[128,4096]{1,0:T(8,128)(2,1)} %value_hbm.1) | copy-start | bytes 3145732
  37.4 1.0 copy-start.5
  42.3 4.9 %collective-permute-start.1 = (f32[16,128]{1,0:T(8,128)S(1)}, f32[16,128]{1,0:T(8,128)S(1)}, u32[]{:S(2)}, u32[]{:S(2)}) collective-permute-start(f32[16,128]{1,0:T(8,128)S(1)} %get-tuple-element.23), channel_id=1, source_target_pairs={{0,32},{32,64},{64,96},{96,0},{1,33},{33,65},{65,97},{97,1},{2,34}... | collective-permute-start | bytes 24584 | tf_op jit(solution)/shard_map/ppermute | solution.py:305
  43.4 5.2 %collective-permute-start.2 = (f32[16,128]{1,0:T(8,128)S(1)}, f32[16,128]{1,0:T(8,128)S(1)}, u32[]{:S(2)}, u32[]{:S(2)}) collective-permute-start(f32[16,128]{1,0:T(8,128)S(1)} %get-tuple-element.23), channel_id=1, source_target_pairs={{0,64},{32,96},{64,0},{96,32},{1,65},{33,97},{65,1},{97,33},{2,66}... | collective-permute-start | bytes 24584 | tf_op jit(solution)/shard_map/ppermute | solution.py:305
  44.5 4.0 %collective-permute-start.3 = (f32[16,128]{1,0:T(8,128)S(1)}, f32[16,128]{1,0:T(8,128)S(1)}, u32[]{:S(2)}, u32[]{:S(2)}) collective-permute-start(f32[16,128]{1,0:T(8,128)S(1)} %get-tuple-element.23), channel_id=1, source_target_pairs={{0,96},{32,0},{64,32},{96,64},{1,97},{33,1},{65,33},{97,65},{2,98}... | collective-permute-start | bytes 24584 | tf_op jit(solution)/shard_map/ppermute | solution.py:305
  48.5 29.8 %collective-permute-start.5 = (bf16[32,128,128]{2,1,0:T(8,128)(2,1)S(1)}, bf16[32,128,128]{2,1,0:T(8,128)(2,1)}, u32[]{:S(2)}, u32[]{:S(2)}) collective-permute-start(bf16[32,128,128]{2,1,0:T(8,128)(2,1)S(1)} %signal.1.signal_ref), channel_id=1, source_target_pairs={{0,64},{32,96},{64,0},{96,32},{1,65},{33,97},{65,1},{97,33},{2,66}... | collective-permute-start | bytes 3145736 | tf_op jit(solution)/shard_map/ppermute | solution.py:305
  50.5 35.4 %copy-start.6 = (bf16[128,4096]{1,0:T(8,128)(2,1)S(1)}, bf16[128,4096]{1,0:T(8,128)(2,1)}, u32[]{:S(2)}) copy-start(bf16[128,4096]{1,0:T(8,128)(2,1)} %copy-done.5) | copy-start | bytes 3145732
  50.6 0.7 copy-start.11
  70.7 7.6 %collective-permute-start.4 = (bf16[32,16,128]{2,1,0:T(8,128)(2,1)S(1)}, bf16[32,16,128]{2,1,0:T(8,128)(2,1)S(1)}, u32[]{:S(2)}, u32[]{:S(2)}) collective-permute-start(bf16[32,16,128]{2,1,0:T(8,128)(2,1)S(1)} %slice.4), channel_id=1, source_target_pairs={{0,64},{32,96},{64,0},{96,32},{1,65},{33,97},{65,1},{97,33},{2,66}... | collective-permute-start | bytes 393224 | tf_op jit(solution)/shard_map/ppermute | solution.py:305
  78.3 15.0 %collective-permute-start.6 = (bf16[128,2048]{1,0:T(8,128)(2,1)S(1)}, bf16[128,2048]{1,0:T(8,128)(2,1)S(1)}, u32[]{:S(2)}, u32[]{:S(2)}) collective-permute-start(bf16[128,2048]{1,0:T(8,128)(2,1)S(1)} %gate_rows.3.first_ref), channel_id=1, source_target_pairs={{0,96},{32,0},{64,32},{96,64},{1,97},{33,1},{65,33},{97,65},{2,98}... | collective-permute-start | bytes 1572872 | tf_op jit(solution)/shard_map/ppermute | solution.py:305
  79.3 16.1 %collective-permute-start.7 = (bf16[128,2048]{1,0:T(8,128)(2,1)S(1)}, bf16[128,2048]{1,0:T(8,128)(2,1)S(1)}, u32[]{:S(2)}, u32[]{:S(2)}) collective-permute-start(bf16[128,2048]{1,0:T(8,128)(2,1)S(1)} %gate_rows.3.first_ref), channel_id=1, source_target_pairs={{0,32},{32,64},{64,96},{96,0},{1,33},{33,65},{65,97},{97,1},{2,34}... | collective-permute-start | bytes 1572872 | tf_op jit(solution)/shard_map/ppermute | solution.py:305
  83.6 21.6 %collective-permute-start.8 = (bf16[128,2048]{1,0:T(8,128)(2,1)S(1)}, bf16[128,2048]{1,0:T(8,128)(2,1)S(1)}, u32[]{:S(2)}, u32[]{:S(2)}) collective-permute-start(bf16[128,2048]{1,0:T(8,128)(2,1)S(1)} %gate_rows.4.second_ref), channel_id=1, source_target_pairs={{0,96},{32,0},{64,32},{96,64},{1,97},{33,1},{65,33},{97,65},{2,98}... | collective-permute-start | bytes 1572872 | tf_op jit(solution)/shard_map/ppermute | solution.py:305
  85.9 19.3 %collective-permute-start.9 = (bf16[128,2048]{1,0:T(8,128)(2,1)S(1)}, bf16[128,2048]{1,0:T(8,128)(2,1)S(1)}, u32[]{:S(2)}, u32[]{:S(2)}) collective-permute-start(bf16[128,2048]{1,0:T(8,128)(2,1)S(1)} %gate_rows.4.second_ref), channel_id=1, source_target_pairs={{0,32},{32,64},{64,96},{96,0},{1,33},{33,65},{65,97},{97,1},{2,34}... | collective-permute-start | bytes 1572872 | tf_op jit(solution)/shard_map/ppermute | solution.py:305
  93.3 0.8 copy-start.7
  95.4 0.9 copy-start.9
  96.3 3.4 %copy-start = (bf16[4096,1024]{1,0:T(8,128)(2,1)S(1)}, bf16[4096,1024]{1,0:T(8,128)(2,1)}, u32[]{:S(2)}) copy-start(bf16[4096,1024]{1,0:T(8,128)(2,1)} %all-gather.2.cloned.1.call-done.matrix_ref) | copy-start | bytes 25165828
  99.7 1.0 copy-start.8
  100.7 1.0 copy-start.10
  101.7 3.4 %copy-start.1 = (bf16[4096,1024]{1,0:T(8,128)(2,1)S(1)}, bf16[4096,1024]{1,0:T(8,128)(2,1)}, u32[]{:S(2)}) copy-start(bf16[4096,1024]{1,0:T(8,128)(2,1)} %all-gather.2.cloned.1.call-done.matrix_ref) | copy-start | bytes 25165828
Sparse Core Ops, SparseCore 0:
  38.5 57.5 all-gather.1

commit v4 on v3

--- a/solution.py
+++ b/solution.py
@@ -313,8 +313,9 @@
     far_query = from_seq(query_rows, 2)
     signal = make_signal(key_rows, value_rows)
     received = to_owners(signal)
-    received, far_query, out_weight = lax.optimization_barrier((received, far_query, out_weight))
+    received, out_weight = lax.optimization_barrier((received, out_weight))
     full_weight = lax.all_gather(out_weight, "chan", axis=0, tiled=True)
+    received, far_query = lax.optimization_barrier((received, far_query))
 
     prefix, total = block_states(tokens, rate, received)
     totals = [from_seq(total, s) for s in (1, 2, 3)]

time: 116 us -> 139 us (1.20); the launches traced: 114 us -> 139 us
  waiting for transfers between devices: 5.95 us -> 28.4 us
  starting transfers between devices: 16.3 us -> 20.3 us
  blocking collectives: 43.2 us -> 41.4 us
    ppermute x10, waiting for transfers between devices: 5.93 us -> 28.3 us  [from_seq(): lax.ppermute(array, 'seq', [(i, (i + s) % seq_count) for i in range(seq_c...]
    ppermute x10, starting transfers between devices: 16.3 us -> 20.3 us  [from_seq(): lax.ppermute(array, 'seq', [(i, (i + s) % seq_count) for i in range(seq_c...]
    all_to_all x2, blocking collectives: 43.2 us -> 41.4 us  [to_owners(): lax.all_to_all(array, 'chan', split_axis=0, concat_axis=0, tiled=True)]
  transfers between devices with their start and end apart: 11 -> 11, of which waited for: 4 -> 5; matrix products, arithmetic and copies ran while one was open for 1% -> 1% of each run, Pallas kernels for 18% -> 15%
where the time goes in v4:
time: 139 us
  blocking collectives  41.4 us (30%)
  waiting for transfers between devices  28.4 us (20%)
  Pallas kernels  23.3 us (17%)
  starting transfers between devices  20.3 us (15%)
  between operations  13.5 us (10%)
  local copies, waits for them, and re-layouts  11.4 us (8%)
    all_to_all x2, blocking collectives, to_owners(): lax.all_to_all(array, 'chan', split_axis=0, concat_axis=0, tiled=True)  41.4 us
    ppermute x10, waiting for transfers between devices, from_seq(): lax.ppermute(array, 'seq', [(i, (i + s) % seq_count) for i in range(seq_c...  28.3 us
    ppermute x10, starting transfers between devices, from_seq(): lax.ppermute(array, 'seq', [(i, (i + s) % seq_count) for i in range(seq_c...  20.3 us
    pallas_call x3, Pallas kernels, gate_rows(): call(gate_kernel, 'gate_rows', moved=moved, grid=(count,), in_specs=[pl.B...  13.9 us
    unnamed x24, local copies, waits for them, and re-layouts  11.4 us
    pallas_call x1, Pallas kernels, early_rows(): call(early_kernel, 'early_rows', in_specs=[whole] * 6, out_specs=[whole]...  3.42 us
    pallas_call x1, Pallas kernels, block_states(): call(functools.partial(states_kernel, tokens), 'block_states', grid=(bloc...  3.16 us
  transfers between devices with their start and end apart: 11, of which 5 were waited for; matrix products, arithmetic and copies ran while one was open for 1% of the time, Pallas kernels for 15%

profile of v4, /device:TPU:0, one launch (start us, length us, event | category | flops | bytes accessed | tf_op | source)
XLA Modules:
  0.0 139.0 jit_solution(13217988743579648073)
XLA Ops:
  6.5 1.3 copy-done.3
  7.9 1.2 copy-done.4
  9.6 24.0 %all_to_all.10.signal_ref = bf16[32,128,128]{2,1,0:T(8,128)(2,1)S(1)} all-to-all(bf16[32,128,128]{2,1,0:T(8,128)(2,1)S(1)} %signal.1.signal_ref), channel_id=1, replica_groups=mesh['seq'=4,'chan'=32] {'chan'}, dimensions={0} | all-to-all | bytes 2097152 | tf_op jit(solution)/shard_map/all_to_all | solution.py:308
  33.6 4.0 %collective-permute-start = (bf16[128,4096]{1,0:T(8,128)(2,1)}, bf16[128,4096]{1,0:T(8,128)(2,1)S(1)}, u32[]{:S(2)}, u32[]{:S(2)}) collective-permute-start(bf16[128,4096]{1,0:T(8,128)(2,1)} %query_ref.3), channel_id=1, source_target_pairs={{0,64},{32,96},{64,0},{96,32},{1,65},{33,97},{65,1},{97,33},{2,66}... | collective-permute-start | bytes 3145736 | tf_op jit(solution)/shard_map/ppermute | solution.py:305
  38.3 23.2 %collective-permute-done.query_ref = bf16[128,4096]{1,0:T(8,128)(2,1)S(1)} collective-permute-done((bf16[128,4096]{1,0:T(8,128)(2,1)}, bf16[128,4096]{1,0:T(8,128)(2,1)S(1)}, u32[]{:S(2)}, u32[]{:S(2)}) %collective-permute-start) | collective-permute-done | bytes 1048608 | tf_op jit(solution)/shard_map/ppermute | solution.py:305
  62.4 3.2 %block_states.1 = (f32[512,128]{1,0:T(8,128)S(1)}, f32[16,128]{1,0:T(8,128)S(1)}) custom-call(f32[16,128]{1,0:T(8,128)S(1)} %get-tuple-element.40.rate_ref, bf16[32,128,128]{2,1,0:T(8,128)(2,1)S(1)} %all_to_all.10.signal_ref), custom_call_target="tpu_custom_call" | custom-call | flops 1024 | bytes 1024 | tf_op jit(solution)/shard_map/block_states/pallas_call | solution.py:117
  65.6 1.4 collective-permute-start.1
  67.0 3.6 %collective-permute-start.2 = (f32[16,128]{1,0:T(8,128)S(1)}, f32[16,128]{1,0:T(8,128)S(1)}, u32[]{:S(2)}, u32[]{:S(2)}) collective-permute-start(f32[16,128]{1,0:T(8,128)S(1)} %get-tuple-element.25), channel_id=1, source_target_pairs={{0,64},{32,96},{64,0},{96,32},{1,65},{33,97},{65,1},{97,33},{2,66}... | collective-permute-start | bytes 24584 | tf_op jit(solution)/shard_map/ppermute | solution.py:305
  72.3 1.9 %collective-permute-done.3.refs_2_ = f32[16,128]{1,0:T(8,128)S(1)} collective-permute-done((f32[16,128]{1,0:T(8,128)S(1)}, f32[16,128]{1,0:T(8,128)S(1)}, u32[]{:S(2)}, u32[]{:S(2)}) %collective-permute-start.3) | collective-permute-done | bytes 8224 | tf_op jit(solution)/shard_map/ppermute | solution.py:305
  74.2 1.5 %collective-permute-start.5 = (bf16[32,128,128]{2,1,0:T(8,128)(2,1)S(1)}, bf16[32,128,128]{2,1,0:T(8,128)(2,1)}, u32[]{:S(2)}, u32[]{:S(2)}) collective-permute-start(bf16[32,128,128]{2,1,0:T(8,128)(2,1)S(1)} %signal.1.signal_ref), channel_id=1, source_target_pairs={{0,64},{32,96},{64,0},{96,32},{1,65},{33,97},{65,1},{97,33},{2,66}... | collective-permute-start | bytes 3145736 | tf_op jit(solution)/shard_map/ppermute | solution.py:305
  76.5 17.4 %all_to_all.11.packed_ref.before_ref = bf16[32,96,128]{2,1,0:T(8,128)(2,1)S(1)} all-to-all(bf16[32,96,128]{2,1,0:T(8,128)(2,1)S(1)} %states_before.1), channel_id=1, replica_groups=mesh['seq'=4,'chan'=32] {'chan'}, dimensions={0} | all-to-all | bytes 1572864 | tf_op jit(solution)/shard_map/all_to_all | solution.py:308
  93.9 3.4 %collective-permute-start.4 = (bf16[32,16,128]{2,1,0:T(8,128)(2,1)S(1)}, bf16[32,16,128]{2,1,0:T(8,128)(2,1)S(1)}, u32[]{:S(2)}, u32[]{:S(2)}) collective-permute-start(bf16[32,16,128]{2,1,0:T(8,128)(2,1)S(1)} %slice.4), channel_id=1, source_target_pairs={{0,64},{32,96},{64,0},{96,32},{1,65},{33,97},{65,1},{97,33},{2,66}... | collective-permute-start | bytes 393224 | tf_op jit(solution)/shard_map/ppermute | solution.py:305
  97.3 3.3 %gate_rows.3.first_ref = bf16[128,2048]{1,0:T(8,128)(2,1)S(1)} custom-call(bf16[32,96,128]{2,1,0:T(8,128)(2,1)S(1)} %all_to_all.11.packed_ref.before_ref, bf16[32,96,128]{2,1,0:T(8,128)(2,1)S(1)} %all_to_all.11.packed_ref.before_ref, bf16[32,128,128]{2,1,0:T(8,128)(2,1)S(1)} %signal.1.signal_ref, bf16[128,4096]{1,0:T(8,128)(2,1)S(1)} %copy-done.2), custom_call_target="tpu_custom_call" | custom-call | flops 1024 | bytes 1024 | tf_op jit(solution)/shard_map/gate_rows/pallas_call | solution.py:212
  100.6 1.2 collective-permute-done.4.before_ref
  101.8 2.2 %collective-permute-start.6 = (bf16[128,2048]{1,0:T(8,128)(2,1)S(1)}, bf16[128,2048]{1,0:T(8,128)(2,1)S(1)}, u32[]{:S(2)}, u32[]{:S(2)}) collective-permute-start(bf16[128,2048]{1,0:T(8,128)(2,1)S(1)} %gate_rows.3.first_ref), channel_id=1, source_target_pairs={{0,96},{32,0},{64,32},{96,64},{1,97},{33,1},{65,33},{97,65},{2,98}... | collective-permute-start | bytes 1572872 | tf_op jit(solution)/shard_map/ppermute | solution.py:305
  104.0 3.3 %gate_rows.4.second_ref = bf16[128,2048]{1,0:T(8,128)(2,1)S(1)} custom-call(bf16[32,96,128]{2,1,0:T(8,128)(2,1)S(1)} %all_to_all.11.packed_ref.before_ref, bf16[32,96,128]{2,1,0:T(8,128)(2,1)S(1)} %all_to_all.11.packed_ref.before_ref, bf16[32,128,128]{2,1,0:T(8,128)(2,1)S(1)} %signal.1.signal_ref, bf16[128,4096]{1,0:T(8,128)(2,1)S(1)} %copy-done.2), custom_call_target="tpu_custom_call" | custom-call | flops 1024 | bytes 1024 | tf_op jit(solution)/shard_map/gate_rows/pallas_call | solution.py:212
  107.3 3.3 %collective-permute-start.8 = (bf16[128,2048]{1,0:T(8,128)(2,1)S(1)}, bf16[128,2048]{1,0:T(8,128)(2,1)S(1)}, u32[]{:S(2)}, u32[]{:S(2)}) collective-permute-start(bf16[128,2048]{1,0:T(8,128)(2,1)S(1)} %gate_rows.4.second_ref), channel_id=1, source_target_pairs={{0,96},{32,0},{64,32},{96,64},{1,97},{33,1},{65,33},{97,65},{2,98}... | collective-permute-start | bytes 1572872 | tf_op jit(solution)/shard_map/ppermute | solution.py:305
  110.6 7.4 %gate_rows.5.far_ref = bf16[128,4096]{1,0:T(8,128)(2,1)S(1)} custom-call(bf16[32,96,128]{2,1,0:T(8,128)(2,1)S(1)} %all_to_all.11.packed_ref.before_ref, bf16[32,16,128]{2,1,0:T(8,128)(2,1)S(1)} %collective-permute-done.4.before_ref, bf16[32,128,128]{2,1,0:T(8,128)(2,1)} %collective-permute-done.5.signal_ref, bf16[128,4096]{1,0:T(8,128)(2,1)S(1)} %copy-done.6), custom_call_target="tpu_custom_call" | custom-call | flops 1024 | bytes 20971520 | tf_op jit(solution)/shard_map/gate_rows/pallas_call | solution.py:212
  118.8 1.3 collective-permute-done.7.lower_ref
  121.0 3.4 %copy-done = bf16[4096,1024]{1,0:T(8,128)(2,1)S(1)} copy-done((bf16[4096,1024]{1,0:T(8,128)(2,1)S(1)}, bf16[4096,1024]{1,0:T(8,128)(2,1)}, u32[]{:S(2)}) %copy-start) | copy-done | bytes 8388632
  124.4 1.0 copy-done.8
  125.4 1.0 copy-done.10
  126.5 3.4 %early_rows.1 = (bf16[256,1024]{1,0:T(8,128)(2,1)S(1)}, f32[256,1024]{1,0:T(8,128)S(1)}) custom-call(bf16[128,2048]{1,0:T(8,128)(2,1)S(1)} %gate_rows.3.first_ref, bf16[128,2048]{1,0:T(8,128)(2,1)S(1)} %gate_rows.4.second_ref, bf16[128,4096]{1,0:T(8,128)(2,1)S(1)} %gate_rows.5.far_ref, bf16[128,2048]{1,0:T(8,128)(2,1)S(1)} %copy-done.8, ...), custom_call_target="tpu_custom_call" | custom-call | flops 1024 | bytes 1024 | tf_op jit(solution)/shard_map/early_rows/pallas_call | solution.py:252
  129.9 2.2 %finish.1 = bf16[4,128,1024]{2,1,0:T(8,128)(2,1)} custom-call(s32[1]{0:T(128)} %bitcast.place_ref, bf16[256,1024]{1,0:T(8,128)(2,1)S(1)} %get-tuple-element.37.done_ref, f32[256,1024]{1,0:T(8,128)S(1)} %get-tuple-element.38.sum_ref, bf16[128,2048]{1,0:T(8,128)(2,1)S(1)} %collective-permute-done.8.upper_ref, ...), custom_call_target="tpu_custom_call" | custom-call | flops 1024 | bytes 1024 | tf_op jit(solution)/shard_map/finish/pallas_call | solution.py:287
  (35 shorter events, 6.4 us)
Async XLA Ops:
  6.5 90.8 %copy-start.2 = (bf16[128,4096]{1,0:T(8,128)(2,1)S(1)}, bf16[128,4096]{1,0:T(8,128)(2,1)}, u32[]{:S(2)}) copy-start(bf16[128,4096]{1,0:T(8,128)(2,1)} %query_ref.3) | copy-start | bytes 3145732
  6.5 114.5 %all-gather.2.cloned.1.call-start = ((), (), s32[]{:S(2)}) async-start(), calls=%async_computation.2 | async-start | bytes 8650752 | tf_op jit(solution)/shard_map/all_gather | solution.py:317
  6.5 1.3 copy-start.3
  7.9 1.2 copy-start.4
  33.6 27.9 %collective-permute-start = (bf16[128,4096]{1,0:T(8,128)(2,1)}, bf16[128,4096]{1,0:T(8,128)(2,1)S(1)}, u32[]{:S(2)}, u32[]{:S(2)}) collective-permute-start(bf16[128,4096]{1,0:T(8,128)(2,1)} %query_ref.3), channel_id=1, source_target_pairs={{0,64},{32,96},{64,0},{96,32},{1,65},{33,97},{65,1},{97,33},{2,66}... | collective-permute-start | bytes 3145736 | tf_op jit(solution)/shard_map/ppermute | solution.py:305
  61.5 1.0 copy-start.5
  65.6 5.9 %collective-permute-start.1 = (f32[16,128]{1,0:T(8,128)S(1)}, f32[16,128]{1,0:T(8,128)S(1)}, u32[]{:S(2)}, u32[]{:S(2)}) collective-permute-start(f32[16,128]{1,0:T(8,128)S(1)} %get-tuple-element.25), channel_id=1, source_target_pairs={{0,32},{32,64},{64,96},{96,0},{1,33},{33,65},{65,97},{97,1},{2,34}... | collective-permute-start | bytes 24584 | tf_op jit(solution)/shard_map/ppermute | solution.py:305
  67.0 5.3 %collective-permute-start.2 = (f32[16,128]{1,0:T(8,128)S(1)}, f32[16,128]{1,0:T(8,128)S(1)}, u32[]{:S(2)}, u32[]{:S(2)}) collective-permute-start(f32[16,128]{1,0:T(8,128)S(1)} %get-tuple-element.25), channel_id=1, source_target_pairs={{0,64},{32,96},{64,0},{96,32},{1,65},{33,97},{65,1},{97,33},{2,66}... | collective-permute-start | bytes 24584 | tf_op jit(solution)/shard_map/ppermute | solution.py:305
  70.5 3.7 %collective-permute-start.3 = (f32[16,128]{1,0:T(8,128)S(1)}, f32[16,128]{1,0:T(8,128)S(1)}, u32[]{:S(2)}, u32[]{:S(2)}) collective-permute-start(f32[16,128]{1,0:T(8,128)S(1)} %get-tuple-element.25), channel_id=1, source_target_pairs={{0,96},{32,0},{64,32},{96,64},{1,97},{33,1},{65,33},{97,65},{2,98}... | collective-permute-start | bytes 24584 | tf_op jit(solution)/shard_map/ppermute | solution.py:305
  74.2 27.6 %collective-permute-start.5 = (bf16[32,128,128]{2,1,0:T(8,128)(2,1)S(1)}, bf16[32,128,128]{2,1,0:T(8,128)(2,1)}, u32[]{:S(2)}, u32[]{:S(2)}) collective-permute-start(bf16[32,128,128]{2,1,0:T(8,128)(2,1)S(1)} %signal.1.signal_ref), channel_id=1, source_target_pairs={{0,64},{32,96},{64,0},{96,32},{1,65},{33,97},{65,1},{97,33},{2,66}... | collective-permute-start | bytes 3145736 | tf_op jit(solution)/shard_map/ppermute | solution.py:305
  75.7 34.9 %copy-start.6 = (bf16[128,4096]{1,0:T(8,128)(2,1)S(1)}, bf16[128,4096]{1,0:T(8,128)(2,1)}, u32[]{:S(2)}) copy-start(bf16[128,4096]{1,0:T(8,128)(2,1)} %copy-done.5) | copy-start | bytes 3145732
  75.7 0.7 copy-start.11
  93.9 7.9 %collective-permute-start.4 = (bf16[32,16,128]{2,1,0:T(8,128)(2,1)S(1)}, bf16[32,16,128]{2,1,0:T(8,128)(2,1)S(1)}, u32[]{:S(2)}, u32[]{:S(2)}) collective-permute-start(bf16[32,16,128]{2,1,0:T(8,128)(2,1)S(1)} %slice.4), channel_id=1, source_target_pairs={{0,64},{32,96},{64,0},{96,32},{1,65},{33,97},{65,1},{97,33},{2,66}... | collective-permute-start | bytes 393224 | tf_op jit(solution)/shard_map/ppermute | solution.py:305
  101.8 16.2 %collective-permute-start.6 = (bf16[128,2048]{1,0:T(8,128)(2,1)S(1)}, bf16[128,2048]{1,0:T(8,128)(2,1)S(1)}, u32[]{:S(2)}, u32[]{:S(2)}) collective-permute-start(bf16[128,2048]{1,0:T(8,128)(2,1)S(1)} %gate_rows.3.first_ref), channel_id=1, source_target_pairs={{0,96},{32,0},{64,32},{96,64},{1,97},{33,1},{65,33},{97,65},{2,98}... | collective-permute-start | bytes 1572872 | tf_op jit(solution)/shard_map/ppermute | solution.py:305
  104.0 16.1 %collective-permute-start.7 = (bf16[128,2048]{1,0:T(8,128)(2,1)S(1)}, bf16[128,2048]{1,0:T(8,128)(2,1)S(1)}, u32[]{:S(2)}, u32[]{:S(2)}) collective-permute-start(bf16[128,2048]{1,0:T(8,128)(2,1)S(1)} %gate_rows.3.first_ref), channel_id=1, source_target_pairs={{0,32},{32,64},{64,96},{96,0},{1,33},{33,65},{65,97},{97,1},{2,34}... | collective-permute-start | bytes 1572872 | tf_op jit(solution)/shard_map/ppermute | solution.py:305
  107.3 22.6 %collective-permute-start.8 = (bf16[128,2048]{1,0:T(8,128)(2,1)S(1)}, bf16[128,2048]{1,0:T(8,128)(2,1)S(1)}, u32[]{:S(2)}, u32[]{:S(2)}) collective-permute-start(bf16[128,2048]{1,0:T(8,128)(2,1)S(1)} %gate_rows.4.second_ref), channel_id=1, source_target_pairs={{0,96},{32,0},{64,32},{96,64},{1,97},{33,1},{65,33},{97,65},{2,98}... | collective-permute-start | bytes 1572872 | tf_op jit(solution)/shard_map/ppermute | solution.py:305
  110.6 19.3 %collective-permute-start.9 = (bf16[128,2048]{1,0:T(8,128)(2,1)S(1)}, bf16[128,2048]{1,0:T(8,128)(2,1)S(1)}, u32[]{:S(2)}, u32[]{:S(2)}) collective-permute-start(bf16[128,2048]{1,0:T(8,128)(2,1)S(1)} %gate_rows.4.second_ref), channel_id=1, source_target_pairs={{0,32},{32,64},{64,96},{96,0},{1,33},{33,65},{65,97},{97,1},{2,34}... | collective-permute-start | bytes 1572872 | tf_op jit(solution)/shard_map/ppermute | solution.py:305
  118.0 0.8 copy-start.7
  120.1 0.9 copy-start.9
  121.0 3.4 %copy-start = (bf16[4096,1024]{1,0:T(8,128)(2,1)S(1)}, bf16[4096,1024]{1,0:T(8,128)(2,1)}, u32[]{:S(2)}) copy-start(bf16[4096,1024]{1,0:T(8,128)(2,1)} %all-gather.2.cloned.1.call-done.matrix_ref) | copy-start | bytes 25165828
  124.4 1.0 copy-start.8
  125.4 1.0 copy-start.10
  126.5 3.4 %copy-start.1 = (bf16[4096,1024]{1,0:T(8,128)(2,1)S(1)}, bf16[4096,1024]{1,0:T(8,128)(2,1)}, u32[]{:S(2)}) copy-start(bf16[4096,1024]{1,0:T(8,128)(2,1)} %all-gather.2.cloned.1.call-done.matrix_ref) | copy-start | bytes 25165828
Sparse Core Ops, SparseCore 0:
  33.7 51.8 all-gather.1

commit v5 on v3

--- a/solution.py
+++ b/solution.py
@@ -16,7 +16,7 @@
 PARAMS = 5 * ORDER
 SMALL_LIMIT = 16 * 1024 * 1024
 LARGE_LIMIT = 56 * 1024 * 1024
-COLUMNS = 256
+COLUMNS = 512
 
 
 def call(kernel, name, limit=SMALL_LIMIT, moved=1024, **keywords):
@@ -230,7 +230,7 @@
     )(packed, before, signal, query)
 
 
-def early_kernel(first_ref, second_ref, far_ref, upper_ref, lower_ref, matrix_ref, done_ref, sum_ref, rows_ref, half_ref):
+def early_kernel(first_ref, second_ref, far_ref, upper_ref, lower_ref, matrix_ref, late_ref, done_ref, sum_ref, rows_ref, half_ref):
     tokens, split = first_ref.shape
     rows_ref[:tokens, :split] = first_ref[...]
     rows_ref[:tokens, split:] = second_ref[...]
@@ -239,20 +239,25 @@
     half_ref[tokens:, :] = lower_ref[...]
     for n in range(0, done_ref.shape[1], COLUMNS):
         columns = slice(n, n + COLUMNS)
-        product = jnp.dot(rows_ref[...], matrix_ref[:, columns], preferred_element_type=jnp.float32)
+        product = jnp.dot(
+            rows_ref[:, :split], matrix_ref[:, columns], preferred_element_type=jnp.float32
+        )
+        product += jnp.dot(
+            rows_ref[:, split:], late_ref[:, columns], preferred_element_type=jnp.float32
+        )
         done_ref[:, columns] = product.astype(jnp.bfloat16)
         sum_ref[:, columns] = jnp.dot(
-            half_ref[...], matrix_ref[:split, columns], preferred_element_type=jnp.float32
+            half_ref[...], late_ref[:, columns], preferred_element_type=jnp.float32
         )
 
 
-def early_rows(first, second, far, upper, lower, matrix):
+def early_rows(first, second, far, upper, lower, matrix, late):
     whole = pl.BlockSpec(memory_space=pltpu.VMEM)
     tokens, columns = far.shape[0], matrix.shape[1]
     return call(
         early_kernel,
         "early_rows",
-        in_specs=[whole] * 6,
+        in_specs=[whole] * 7,
         out_specs=[whole] * 2,
         out_shape=[
             jax.ShapeDtypeStruct((2 * tokens, columns), jnp.bfloat16),
@@ -262,11 +267,11 @@
             pltpu.VMEM((2 * tokens, far.shape[1]), jnp.bfloat16),
             pltpu.VMEM((2 * tokens, first.shape[1]), jnp.bfloat16),
         ],
-    )(first, second, far, upper, lower, matrix)
+    )(first, second, far, upper, lower, matrix, late)
 
 
 def finish_kernel(place_ref, done_ref, sum_ref, upper_ref, lower_ref, matrix_ref, out_ref, rows_ref):
-    tokens, depth = upper_ref.shape
+    tokens = upper_ref.shape[0]
     rows_ref[:tokens, :] = upper_ref[...]
     rows_ref[tokens:, :] = lower_ref[...]
     own, up, far, low = [lax.rem(place_ref[0] + r, 4) for r in range(4)]
@@ -274,8 +279,7 @@
     out_ref[far] = done_ref[tokens:, :]
     for n in range(0, out_ref.shape[2], COLUMNS):
         columns = slice(n, n + COLUMNS)
-        matrix = matrix_ref[matrix_ref.shape[0] - depth :, columns]
-        product = jnp.dot(rows_ref[...], matrix, preferred_element_type=jnp.float32)
+        product = jnp.dot(rows_ref[...], matrix_ref[:, columns], preferred_element_type=jnp.float32)
         total = (sum_ref[:, columns] + product).astype(jnp.bfloat16)
         out_ref[up, :, columns] = total[:tokens]
         out_ref[low, :, columns] = total[tokens:]
@@ -330,8 +334,10 @@
     low_second, up_second = from_seq(second, 1), from_seq(second, -1)
     second, far_before = lax.optimization_barrier((second, far_before))
     far = gate_rows(packed, far_before, far_signal, far_query, 0, 2 * half, 20 * 1024 * 1024)
-    done, early_sum = early_rows(first, second, far, up_first, low_first, full_weight)
-    return finish(z, done, early_sum, up_second, low_second, full_weight)
+    split = half * GROUP
+    soon, late = full_weight[:split], full_weight[split:]
+    done, early_sum = early_rows(first, second, far, up_second, low_second, soon, late)
+    return finish(z, done, early_sum, up_first, low_first, soon)
 
 
 def solution(mesh):

time: 116 us -> 116 us (level)
  local copies, waits for them, and re-layouts: 11.3 us -> 7.38 us
  waiting for transfers between devices: 5.95 us -> 7.64 us
  Pallas kernels: 23.3 us -> 24.6 us
    unnamed x24 -> x16, local copies, waits for them, and re-layouts: 11.3 us -> 3.44 us
    slice x0 -> x1, local copies, waits for them, and re-layouts: none -> 3.93 us  [on_device(): soon, late = (full_weight[:split], full_weight[split:])]
    all_gather x1, waiting for transfers between devices: 0.01 us -> 2.75 us  [on_device(): full_weight = lax.all_gather(out_weight, 'chan', axis=0, tiled=True)]
    pallas_call x1, Pallas kernels: 3.42 us -> 4.65 us  [early_rows(): call(early_kernel, 'early_rows', in_specs=[whole] * 7, out_specs=[whole]...]
  transfers between devices with their start and end apart: 11 -> 11, of which waited for: 4 -> 4; matrix products, arithmetic and copies ran while one was open for 1% -> 3% of each run, Pallas kernels for 18% -> 20%
where the time goes in v5:
time: 116 us; the launch traced here: 114 us
  blocking collectives  43.7 us (38%)
  Pallas kernels  24.6 us (21%)
  starting transfers between devices  17.3 us (15%)
  between operations  13.6 us (12%)
  waiting for transfers between devices  7.64 us (7%)
  local copies, waits for them, and re-layouts  7.38 us (6%)
    all_to_all x2, blocking collectives, to_owners(): lax.all_to_all(array, 'chan', split_axis=0, concat_axis=0, tiled=True)  43.7 us
    ppermute x10, starting transfers between devices, from_seq(): lax.ppermute(array, 'seq', [(i, (i + s) % seq_count) for i in range(seq_c...  17.3 us
    pallas_call x3, Pallas kernels, gate_rows(): call(gate_kernel, 'gate_rows', moved=moved, grid=(count,), in_specs=[pl.B...  13.9 us
    ppermute x10, waiting for transfers between devices, from_seq(): lax.ppermute(array, 'seq', [(i, (i + s) % seq_count) for i in range(seq_c...  4.88 us
    pallas_call x1, Pallas kernels, early_rows(): call(early_kernel, 'early_rows', in_specs=[whole] * 7, out_specs=[whole]...  4.65 us
    slice x1, local copies, waits for them, and re-layouts, on_device(): soon, late = (full_weight[:split], full_weight[split:])  3.93 us
    unnamed x16, local copies, waits for them, and re-layouts  3.44 us
    pallas_call x1, Pallas kernels, block_states(): call(functools.partial(states_kernel, tokens), 'block_states', grid=(bloc...  3.18 us
  transfers between devices with their start and end apart: 11, of which 4 were waited for; matrix products, arithmetic and copies ran while one was open for 3% of the time, Pallas kernels for 20%

profile of v5, /device:TPU:0, one launch (start us, length us, event | category | flops | bytes accessed | tf_op | source)
XLA Modules:
  0.0 114.1 jit_solution(7049026584490248311)
XLA Ops:
  6.5 4.0 %collective-permute-start = (bf16[128,4096]{1,0:T(8,128)(2,1)}, bf16[128,4096]{1,0:T(8,128)(2,1)S(1)}, u32[]{:S(2)}, u32[]{:S(2)}) collective-permute-start(bf16[128,4096]{1,0:T(8,128)(2,1)} %query_ref.3), channel_id=1, source_target_pairs={{0,64},{32,96},{64,0},{96,32},{1,65},{33,97},{65,1},{97,33},{2,66}... | collective-permute-start | bytes 3145736 | tf_op jit(solution)/shard_map/ppermute | solution.py:309
  10.5 1.2 %copy-done.1 = bf16[128,4096]{1,0:T(8,128)(2,1)S(1)} copy-done((bf16[128,4096]{1,0:T(8,128)(2,1)S(1)}, bf16[128,4096]{1,0:T(8,128)(2,1)}, u32[]{:S(2)}) %copy-start.1) | copy-done | bytes 1048600
  11.7 1.2 %copy-done.2 = bf16[128,4096]{1,0:T(8,128)(2,1)S(1)} copy-done((bf16[128,4096]{1,0:T(8,128)(2,1)S(1)}, bf16[128,4096]{1,0:T(8,128)(2,1)}, u32[]{:S(2)}) %copy-start.2) | copy-done | bytes 1048600
  13.0 0.5 signal.1.signal_ref
  13.4 23.9 %all_to_all.10.signal_ref = bf16[32,128,128]{2,1,0:T(8,128)(2,1)S(1)} all-to-all(bf16[32,128,128]{2,1,0:T(8,128)(2,1)S(1)} %signal.1.signal_ref), channel_id=1, replica_groups=mesh['seq'=4,'chan'=32] {'chan'}, dimensions={0} | all-to-all | bytes 2097152 | tf_op jit(solution)/shard_map/all_to_all | solution.py:312
  37.4 1.0 copy-done.3
  38.4 3.2 %block_states.1 = (f32[512,128]{1,0:T(8,128)S(1)}, f32[16,128]{1,0:T(8,128)S(1)}) custom-call(f32[16,128]{1,0:T(8,128)S(1)} %get-tuple-element.40.rate_ref, bf16[32,128,128]{2,1,0:T(8,128)(2,1)S(1)} %all_to_all.10.signal_ref), custom_call_target="tpu_custom_call" | custom-call | flops 1024 | bytes 1024 | tf_op jit(solution)/shard_map/block_states/pallas_call | solution.py:117
  41.6 0.8 collective-permute-start.3
  42.4 2.4 %collective-permute-start.2 = (f32[16,128]{1,0:T(8,128)S(1)}, f32[16,128]{1,0:T(8,128)S(1)}, u32[]{:S(2)}, u32[]{:S(2)}) collective-permute-start(f32[16,128]{1,0:T(8,128)S(1)} %get-tuple-element.23), channel_id=1, source_target_pairs={{0,64},{32,96},{64,0},{96,32},{1,65},{33,97},{65,1},{97,33},{2,66}... | collective-permute-start | bytes 24584 | tf_op jit(solution)/shard_map/ppermute | solution.py:309
  44.8 0.6 collective-permute-done.3.refs_2_
  45.3 2.2 %collective-permute-done.2.refs_1_ = f32[16,128]{1,0:T(8,128)S(1)} collective-permute-done((f32[16,128]{1,0:T(8,128)S(1)}, f32[16,128]{1,0:T(8,128)S(1)}, u32[]{:S(2)}, u32[]{:S(2)}) %collective-permute-start.2) | collective-permute-done | bytes 8224 | tf_op jit(solution)/shard_map/ppermute | solution.py:309
  47.5 2.1 %collective-permute-done.1.refs_0_ = f32[16,128]{1,0:T(8,128)S(1)} collective-permute-done((f32[16,128]{1,0:T(8,128)S(1)}, f32[16,128]{1,0:T(8,128)S(1)}, u32[]{:S(2)}, u32[]{:S(2)}) %collective-permute-start.1) | collective-permute-done | bytes 8224 | tf_op jit(solution)/shard_map/ppermute | solution.py:309
  49.6 0.3 collective-permute-start.5
  50.0 19.8 %all_to_all.11.packed_ref.before_ref = bf16[32,96,128]{2,1,0:T(8,128)(2,1)S(1)} all-to-all(bf16[32,96,128]{2,1,0:T(8,128)(2,1)S(1)} %states_before.1), channel_id=1, replica_groups=mesh['seq'=4,'chan'=32] {'chan'}, dimensions={0} | all-to-all | bytes 1572864 | tf_op jit(solution)/shard_map/all_to_all | solution.py:312
  69.8 3.2 %collective-permute-start.4 = (bf16[32,16,128]{2,1,0:T(8,128)(2,1)S(1)}, bf16[32,16,128]{2,1,0:T(8,128)(2,1)S(1)}, u32[]{:S(2)}, u32[]{:S(2)}) collective-permute-start(bf16[32,16,128]{2,1,0:T(8,128)(2,1)S(1)} %slice.12), channel_id=1, source_target_pairs={{0,64},{32,96},{64,0},{96,32},{1,65},{33,97},{65,1},{97,33},{2,66}... | collective-permute-start | bytes 393224 | tf_op jit(solution)/shard_map/ppermute | solution.py:309
  73.0 3.3 %gate_rows.4.second_ref = bf16[128,2048]{1,0:T(8,128)(2,1)S(1)} custom-call(bf16[32,96,128]{2,1,0:T(8,128)(2,1)S(1)} %all_to_all.11.packed_ref.before_ref, bf16[32,96,128]{2,1,0:T(8,128)(2,1)S(1)} %all_to_all.11.packed_ref.before_ref, bf16[32,128,128]{2,1,0:T(8,128)(2,1)S(1)} %signal.1.signal_ref, bf16[128,4096]{1,0:T(8,128)(2,1)S(1)} %copy-done), custom_call_target="tpu_custom_call" | custom-call | flops 1024 | bytes 1024 | tf_op jit(solution)/shard_map/gate_rows/pallas_call | solution.py:212
  76.4 3.2 %collective-permute-start.6 = (bf16[128,2048]{1,0:T(8,128)(2,1)S(1)}, bf16[128,2048]{1,0:T(8,128)(2,1)}, u32[]{:S(2)}, u32[]{:S(2)}) collective-permute-start(bf16[128,2048]{1,0:T(8,128)(2,1)S(1)} %gate_rows.4.second_ref), channel_id=1, source_target_pairs={{0,96},{32,0},{64,32},{96,64},{1,97},{33,1},{65,33},{97,65},{2,98}... | collective-permute-start | bytes 1572872 | tf_op jit(solution)/shard_map/ppermute | solution.py:309
  79.6 3.3 %gate_rows.3.first_ref = bf16[128,2048]{1,0:T(8,128)(2,1)S(1)} custom-call(bf16[32,96,128]{2,1,0:T(8,128)(2,1)S(1)} %all_to_all.11.packed_ref.before_ref, bf16[32,96,128]{2,1,0:T(8,128)(2,1)S(1)} %all_to_all.11.packed_ref.before_ref, bf16[32,128,128]{2,1,0:T(8,128)(2,1)S(1)} %signal.1.signal_ref, bf16[128,4096]{1,0:T(8,128)(2,1)S(1)} %copy-done), custom_call_target="tpu_custom_call" | custom-call | flops 1024 | bytes 1024 | tf_op jit(solution)/shard_map/gate_rows/pallas_call | solution.py:212
  83.0 3.2 %collective-permute-start.8 = (bf16[128,2048]{1,0:T(8,128)(2,1)S(1)}, bf16[128,2048]{1,0:T(8,128)(2,1)S(1)}, u32[]{:S(2)}, u32[]{:S(2)}) collective-permute-start(bf16[128,2048]{1,0:T(8,128)(2,1)S(1)} %gate_rows.3.first_ref), channel_id=1, source_target_pairs={{0,96},{32,0},{64,32},{96,64},{1,97},{33,1},{65,33},{97,65},{2,98}... | collective-permute-start | bytes 1572872 | tf_op jit(solution)/shard_map/ppermute | solution.py:309
  86.2 7.4 %gate_rows.5.far_ref = bf16[128,4096]{1,0:T(8,128)(2,1)S(1)} custom-call(bf16[32,96,128]{2,1,0:T(8,128)(2,1)S(1)} %all_to_all.11.packed_ref.before_ref, bf16[32,16,128]{2,1,0:T(8,128)(2,1)S(1)} %collective-permute-done.4.before_ref, bf16[32,128,128]{2,1,0:T(8,128)(2,1)} %collective-permute-done.5.signal_ref, bf16[128,4096]{1,0:T(8,128)(2,1)S(1)} %copy-done.4), custom_call_target="tpu_custom_call" | custom-call | flops 1024 | bytes 20971520 | tf_op jit(solution)/shard_map/gate_rows/pallas_call | solution.py:212
  93.6 2.7 %all-gather.2.cloned.1.call-done = bf16[4096,1024]{1,0:T(8,128)(2,1)} async-done(((bf16[128,1024]{1,0:T(8,128)(2,1)}), bf16[4096,1024]{1,0:T(8,128)(2,1)}) %all-gather.2.cloned.1.call-update) | async-done | bytes 8388624 | tf_op jit(solution)/shard_map/all_gather | solution.py:321
  96.4 3.9 %fusion = (bf16[2048,1024]{1,0:T(8,128)(2,1)S(1)}, bf16[2048,1024]{1,0:T(8,128)(2,1)S(1)}) fusion(bf16[4096,1024]{1,0:T(8,128)(2,1)} %all-gather.2.cloned.1.call-done), kind=kLoop, calls=%fused_computation.2 | loop fusion | bytes 16777216 | tf_op jit(solution)/shard_map/slice | solution.py:338
  100.3 4.7 %early_rows.1 = (bf16[256,1024]{1,0:T(8,128)(2,1)S(1)}, f32[256,1024]{1,0:T(8,128)S(1)}) custom-call(bf16[128,2048]{1,0:T(8,128)(2,1)S(1)} %gate_rows.3.first_ref, bf16[128,2048]{1,0:T(8,128)(2,1)S(1)} %gate_rows.4.second_ref, bf16[128,4096]{1,0:T(8,128)(2,1)S(1)} %gate_rows.5.far_ref, bf16[128,2048]{1,0:T(8,128)(2,1)} %collective-permute-done.6.upper_ref, ...), custom_call_target="tpu_custom_call" | custom-call | flops 1024 | bytes 1024 | tf_op jit(solution)/shard_map/early_rows/pallas_call | solution.py:257
  105.0 2.3 %finish.1 = bf16[4,128,1024]{2,1,0:T(8,128)(2,1)} custom-call(s32[1]{0:T(128)} %bitcast.place_ref, bf16[256,1024]{1,0:T(8,128)(2,1)S(1)} %get-tuple-element.35.done_ref, f32[256,1024]{1,0:T(8,128)S(1)} %get-tuple-element.36.sum_ref, bf16[128,2048]{1,0:T(8,128)(2,1)S(1)} %collective-permute-done.8.upper_ref, ...), custom_call_target="tpu_custom_call" | custom-call | flops 1024 | bytes 1024 | tf_op jit(solution)/shard_map/finish/pallas_call | solution.py:291
  (28 shorter events, 0.3 us)
Async XLA Ops:
  6.5 66.5 %copy-start = (bf16[128,4096]{1,0:T(8,128)(2,1)S(1)}, bf16[128,4096]{1,0:T(8,128)(2,1)}, u32[]{:S(2)}) copy-start(bf16[128,4096]{1,0:T(8,128)(2,1)} %query_ref.3) | copy-start | bytes 3145732
  6.5 89.9 %all-gather.2.cloned.1.call-start = ((), (), s32[]{:S(2)}) async-start(), calls=%async_computation.2 | async-start | bytes 8650752 | tf_op jit(solution)/shard_map/all_gather | solution.py:321
  6.5 30.8 %collective-permute-start = (bf16[128,4096]{1,0:T(8,128)(2,1)}, bf16[128,4096]{1,0:T(8,128)(2,1)S(1)}, u32[]{:S(2)}, u32[]{:S(2)}) collective-permute-start(bf16[128,4096]{1,0:T(8,128)(2,1)} %query_ref.3), channel_id=1, source_target_pairs={{0,64},{32,96},{64,0},{96,32},{1,65},{33,97},{65,1},{97,33},{2,66}... | collective-permute-start | bytes 3145736 | tf_op jit(solution)/shard_map/ppermute | solution.py:309
  10.5 1.2 %copy-start.1 = (bf16[128,4096]{1,0:T(8,128)(2,1)S(1)}, bf16[128,4096]{1,0:T(8,128)(2,1)}, u32[]{:S(2)}) copy-start(bf16[128,4096]{1,0:T(8,128)(2,1)} %key_hbm.1) | copy-start | bytes 3145732
  11.7 1.2 %copy-start.2 = (bf16[128,4096]{1,0:T(8,128)(2,1)S(1)}, bf16[128,4096]{1,0:T(8,128)(2,1)}, u32[]{:S(2)}) copy-start(bf16[128,4096]{1,0:T(8,128)(2,1)} %value_hbm.1) | copy-start | bytes 3145732
  12.9 25.4 %copy-start.6 = (f32[128,16]{0,1:T(8,128)S(1)}, f32[128,16]{0,1:T(8,128)}, u32[]{:S(2)}) copy-start(f32[128,16]{0,1:T(8,128)} %param.10) | copy-start | bytes 24580
  13.0 25.4 %copy-start.7 = (f32[128,16]{0,1:T(8,128)S(1)}, f32[128,16]{0,1:T(8,128)}, u32[]{:S(2)}) copy-start(f32[128,16]{0,1:T(8,128)} %param.11) | copy-start | bytes 24580
  13.0 37.0 %copy-start.5 = (f32[128]{0:T(128)S(1)}, f32[128]{0:T(128)}, u32[]{:S(2)}) copy-start(f32[128]{0:T(128)} %param.12) | copy-start | bytes 1540
  37.4 1.0 copy-start.3
  41.6 3.7 %collective-permute-start.3 = (f32[16,128]{1,0:T(8,128)S(1)}, f32[16,128]{1,0:T(8,128)S(1)}, u32[]{:S(2)}, u32[]{:S(2)}) collective-permute-start(f32[16,128]{1,0:T(8,128)S(1)} %get-tuple-element.23), channel_id=1, source_target_pairs={{0,96},{32,0},{64,32},{96,64},{1,97},{33,1},{65,33},{97,65},{2,98}... | collective-permute-start | bytes 24584 | tf_op jit(solution)/shard_map/ppermute | solution.py:309
  42.4 5.2 %collective-permute-start.2 = (f32[16,128]{1,0:T(8,128)S(1)}, f32[16,128]{1,0:T(8,128)S(1)}, u32[]{:S(2)}, u32[]{:S(2)}) collective-permute-start(f32[16,128]{1,0:T(8,128)S(1)} %get-tuple-element.23), channel_id=1, source_target_pairs={{0,64},{32,96},{64,0},{96,32},{1,65},{33,97},{65,1},{97,33},{2,66}... | collective-permute-start | bytes 24584 | tf_op jit(solution)/shard_map/ppermute | solution.py:309
  44.8 4.9 %collective-permute-start.1 = (f32[16,128]{1,0:T(8,128)S(1)}, f32[16,128]{1,0:T(8,128)S(1)}, u32[]{:S(2)}, u32[]{:S(2)}) collective-permute-start(f32[16,128]{1,0:T(8,128)S(1)} %get-tuple-element.23), channel_id=1, source_target_pairs={{0,32},{32,64},{64,96},{96,0},{1,33},{33,65},{65,97},{97,1},{2,34}... | collective-permute-start | bytes 24584 | tf_op jit(solution)/shard_map/ppermute | solution.py:309
  49.6 33.3 %collective-permute-start.5 = (bf16[32,128,128]{2,1,0:T(8,128)(2,1)S(1)}, bf16[32,128,128]{2,1,0:T(8,128)(2,1)}, u32[]{:S(2)}, u32[]{:S(2)}) collective-permute-start(bf16[32,128,128]{2,1,0:T(8,128)(2,1)S(1)} %signal.1.signal_ref), channel_id=1, source_target_pairs={{0,64},{32,96},{64,0},{96,32},{1,65},{33,97},{65,1},{97,33},{2,66}... | collective-permute-start | bytes 3145736 | tf_op jit(solution)/shard_map/ppermute | solution.py:309
  69.8 16.4 %copy-start.4 = (bf16[128,4096]{1,0:T(8,128)(2,1)S(1)}, bf16[128,4096]{1,0:T(8,128)(2,1)}, u32[]{:S(2)}) copy-start(bf16[128,4096]{1,0:T(8,128)(2,1)} %copy-done.3) | copy-start | bytes 3145732
  69.8 13.1 %collective-permute-start.4 = (bf16[32,16,128]{2,1,0:T(8,128)(2,1)S(1)}, bf16[32,16,128]{2,1,0:T(8,128)(2,1)S(1)}, u32[]{:S(2)}, u32[]{:S(2)}) collective-permute-start(bf16[32,16,128]{2,1,0:T(8,128)(2,1)S(1)} %slice.12), channel_id=1, source_target_pairs={{0,64},{32,96},{64,0},{96,32},{1,65},{33,97},{65,1},{97,33},{2,66}... | collective-permute-start | bytes 393224 | tf_op jit(solution)/shard_map/ppermute | solution.py:309
  76.3 24.0 %collective-permute-start.7 = (bf16[128,2048]{1,0:T(8,128)(2,1)S(1)}, bf16[128,2048]{1,0:T(8,128)(2,1)}, u32[]{:S(2)}, u32[]{:S(2)}) collective-permute-start(bf16[128,2048]{1,0:T(8,128)(2,1)S(1)} %gate_rows.4.second_ref), channel_id=1, source_target_pairs={{0,32},{32,64},{64,96},{96,0},{1,33},{33,65},{65,97},{97,1},{2,34}... | collective-permute-start | bytes 1572872 | tf_op jit(solution)/shard_map/ppermute | solution.py:309
  76.4 23.9 %collective-permute-start.6 = (bf16[128,2048]{1,0:T(8,128)(2,1)S(1)}, bf16[128,2048]{1,0:T(8,128)(2,1)}, u32[]{:S(2)}, u32[]{:S(2)}) collective-permute-start(bf16[128,2048]{1,0:T(8,128)(2,1)S(1)} %gate_rows.4.second_ref), channel_id=1, source_target_pairs={{0,96},{32,0},{64,32},{96,64},{1,97},{33,1},{65,33},{97,65},{2,98}... | collective-permute-start | bytes 1572872 | tf_op jit(solution)/shard_map/ppermute | solution.py:309
  82.9 22.1 %collective-permute-start.9 = (bf16[128,2048]{1,0:T(8,128)(2,1)S(1)}, bf16[128,2048]{1,0:T(8,128)(2,1)S(1)}, u32[]{:S(2)}, u32[]{:S(2)}) collective-permute-start(bf16[128,2048]{1,0:T(8,128)(2,1)S(1)} %gate_rows.3.first_ref), channel_id=1, source_target_pairs={{0,32},{32,64},{64,96},{96,0},{1,33},{33,65},{65,97},{97,1},{2,34}... | collective-permute-start | bytes 1572872 | tf_op jit(solution)/shard_map/ppermute | solution.py:309
  83.0 22.0 %collective-permute-start.8 = (bf16[128,2048]{1,0:T(8,128)(2,1)S(1)}, bf16[128,2048]{1,0:T(8,128)(2,1)S(1)}, u32[]{:S(2)}, u32[]{:S(2)}) collective-permute-start(bf16[128,2048]{1,0:T(8,128)(2,1)S(1)} %gate_rows.3.first_ref), channel_id=1, source_target_pairs={{0,96},{32,0},{64,32},{96,64},{1,97},{33,1},{65,33},{97,65},{2,98}... | collective-permute-start | bytes 1572872 | tf_op jit(solution)/shard_map/ppermute | solution.py:309
Sparse Core Ops, SparseCore 0:
  38.5 57.8 all-gather.1
